TPU v7x, 32 devices: a whole 2x2x4 slice. The times are simulated.
32 devices in a mesh: bx: 8 (over z, x), by: 4 (over y, core).
Axes of the slice: x: 2, y: 2, z: 4, core: 2. Of those that a mesh axis runs over, the one named last changes fastest.
Arguments:
- brick_ids: int32 [4096, 3], P(('bx', 'by')), may hold values from 0 to 63, all different within a row; in each aligned block of 128 rows (0 to 127, 128 to 255, ...) at most 18 rows name the same one
- cell_index: int32 [6, 3, 3, 4096], P(None, None, None, ('bx', 'by')), may hold values from 0 to 14
- cell_frac: float32 [6, 3, 3, 4096], P(None, None, None, ('bx', 'by')), may hold values from 0 to 1
- step_length: float32 [3, 3, 4096], P(None, None, ('bx', 'by')), may hold values from 0.01 to 0.05
- target: float32 [3, 4096], P(None, ('bx', 'by')), may hold values from 0 to 1
- planes: bfloat16 [64, 3, 256, 128], P(('bx', 'by')), may hold values from -6 to 6
- first_layer: bfloat16 [64, 128, 256], P(('bx', 'by')), may hold values from -0.5 to 0.5
- last_layer: bfloat16 [64, 4, 256], P(('bx', 'by')), may hold values from -0.375 to 0.375
Outputs:
- colour: float32 [3, 4096], P(None, ('bx', 'by'))
- plane_grad: float32 [64, 3, 256, 128], P(('bx', 'by'))
- first_grad: float32 [64, 128, 256], P(('bx', 'by'))
- last_grad: float32 [64, 4, 256], P(('bx', 'by'))
Inputs may be any that keep to these rules, and one draw needn't show every extreme that they name: `brick_ids`: row r lists the 3 different bricks that ray r crosses, in the order in which it crosses them; among the rays of one device no brick is named more than 18 times.
All inputs are finite; a program needn't handle non-finite values.
Results may differ from a plain program's by a relative error of at most 0.007.
The roundings to bfloat16 on the way count: a program that leaves them out, or rounds other values in their place, can miss the bound.
Values sent between devices are 32-bit elements; how exact they have to be, the bound alone decides.
A program may use at most 64 MiB of HBM per device.

v0:
```python
import functools

import jax
import jax.numpy as jnp
from jax import lax
from jax.experimental import pallas as pl
from jax.experimental.pallas import tpu as pltpu
from jax.sharding import PartitionSpec as P

MESH = pl.DeviceIdType.MESH
F32 = jnp.float32
BF16 = jnp.bfloat16
LANES = 128
ROWS = 8
GROUP = 8


def matmul(lhs, rhs, contract):
    return lax.dot_general(lhs, rhs, (contract, ((), ())), preferred_element_type=F32)


def exact_parts(value):
    high = value.astype(BF16).astype(F32)
    rest = value - high
    middle = rest.astype(BF16).astype(F32)
    return high, middle, rest - middle


def pair_merge(even, odd, low_lanes):
    half = LANES // 2
    first = jnp.where(low_lanes, even, pltpu.roll(odd, half, 1))
    second = jnp.where(low_lanes, pltpu.roll(even, half, 1), odd)
    return first, second


def step_kernel(
    along_x, along_y, capacity,
    ids_ref, cell_ref, frac_ref, step_ref, target_ref, planes_ref, first_ref, last_ref,
    colour_ref, plane_grad_ref, first_grad_ref, last_grad_ref,
    payload, target_tile, last_wide,
    out_a, in_a, out_b, in_b, out_c, in_c,
    planes_t, first_t, corner, feature, hidden, slope, last_total,
    send_sem, recv_sem,
):
    count = along_x * along_y
    bricks, orients, cells, channels = planes_ref.shape
    side = 1
    while side * side < cells:
        side = side * 2
    crossed, samples, rays = step_ref.shape
    points = crossed * samples
    total = points * rays
    segments = crossed * rays
    half = LANES // bricks
    all_bricks = bricks * count
    chunk = GROUP * half
    chunks = count // GROUP
    me = lax.axis_index("bx") * along_y + lax.axis_index("by")

    def device(number):
        return (lax.div(number, along_y), lax.rem(number, along_y))

    def ahead(offset):
        return device(lax.rem(me + offset, count))

    def behind(offset):
        return device(lax.rem(me + count - offset, count))

    def transfer(phase, source, landing, offset, peer):
        return pltpu.make_async_remote_copy(
            src_ref=source.at[offset],
            dst_ref=landing.at[offset],
            send_sem=send_sem.at[phase, offset],
            recv_sem=recv_sem.at[phase, offset],
            device_id=peer,
            device_id_type=MESH,
        )

    barrier = pltpu.get_barrier_semaphore()

    def greet(offset, carry):
        pl.semaphore_signal(barrier, inc=1, device_id=ahead(offset), device_id_type=MESH)
        return carry

    lax.fori_loop(1, count, greet, 0)

    ids = [ids_ref[pl.ds(k, 1), :] for k in range(crossed)]
    ids_row = jnp.concatenate(ids, axis=1)
    member = lax.broadcasted_iota(jnp.int32, (all_bricks, segments), 0) == ids_row
    member_f = jnp.where(member, 1.0, 0.0).astype(F32)
    earlier = lax.broadcasted_iota(jnp.int32, (segments, segments), 0) < lax.broadcasted_iota(
        jnp.int32, (segments, segments), 1
    )
    ranks = matmul(
        member_f.astype(BF16), jnp.where(earlier, 1.0, 0.0).astype(BF16), ((1,), (0,))
    )
    ranking = jnp.sum(member_f * ranks, axis=0, keepdims=True).astype(jnp.int32)
    shift = bricks.bit_length() - 1
    away = lax.shift_right_logical(ids_row, shift) - me
    away = jnp.where(away < 0, away + count, away)
    place = (ids_row & (bricks - 1)) * half + ranking
    away_all, place_all = [], []
    for k in range(crossed):
        block = slice(k * rays, (k + 1) * rays)
        for s in range(samples):
            away_all.append(away[:, block])
            place_all.append(place[:, block] + s * capacity)
    away_all = jnp.concatenate(away_all, axis=1)
    place_all = jnp.concatenate(place_all, axis=1)
    lane_hot = jnp.where(
        lax.broadcasted_iota(jnp.int32, (LANES, total), 0) == place_all, 1.0, 0.0
    ).astype(BF16)
    chosen = lax.broadcasted_iota(jnp.int32, (count, ROWS, total), 0) == away_all[None]

    def scatter(value):
        tiles = jnp.zeros((count * ROWS, LANES), F32)
        for part in exact_parts(value):
            spread = jnp.where(chosen, part[None], 0.0).reshape(count * ROWS, total).astype(BF16)
            tiles = tiles + matmul(spread, lane_hot, ((1,), (1,)))
        return tiles.reshape(count, ROWS, LANES)

    payload[...] = jnp.zeros_like(payload)
    for k in range(crossed):
        for s in range(samples):
            lanes = pl.ds((k * samples + s) * rays, rays)
            for axis in range(2 * orients):
                payload[pl.ds(axis, 1), lanes] = (
                    cell_ref[axis, k, pl.ds(s, 1), :].astype(F32)
                    + frac_ref[axis, k, pl.ds(s, 1), :]
                )
    tiles = scatter(payload[...])
    out_a[...] = tiles
    in_a[0] = tiles[0]

    pl.semaphore_wait(barrier, count - 1)

    def send_a(offset, carry):
        transfer(0, out_a, in_a, offset, ahead(offset)).start()
        return carry

    lax.fori_loop(1, count, send_a, 0)

    for b in range(bricks):
        for orient in range(orients):
            planes_t[b, :, pl.ds(orient * cells, cells)] = planes_ref[b, orient].T
        first_t[b] = first_ref[b].T
    last_wide[...] = jnp.zeros_like(last_wide)
    for b in range(bricks):
        last_wide[b, pl.ds(0, 4), :] = last_ref[b].astype(F32)
    target_tile[...] = jnp.zeros_like(target_tile)
    target_tile[pl.ds(1, 3), :] = target_ref[...]

    low_lanes = lax.broadcasted_iota(jnp.int32, (ROWS, LANES), 1) < half
    row = lax.broadcasted_iota(jnp.int32, (ROWS, LANES), 0)
    lines = lax.broadcasted_iota(jnp.int32, (side, chunk), 0).astype(F32)
    chunk_row = lax.broadcasted_iota(jnp.int32, (ROWS, chunk), 0)

    def arrive(phase, source, landing, peer, start):
        def wait(offset, carry):
            transfer(phase, source, landing, offset, peer(offset)).wait_recv()
            return carry

        lax.fori_loop(jnp.maximum(start, 1), start + GROUP, wait, 0)

    def split_bricks(landing, start):
        held = [[] for _ in range(bricks)]
        for pair in range(GROUP // 2):
            merged = pair_merge(
                landing[start + 2 * pair], landing[start + 2 * pair + 1], low_lanes
            )
            for b in range(bricks):
                held[b].append(merged[b])
        return [jnp.concatenate(part, axis=1) for part in held]

    def forward(step, carry):
        start = step * GROUP
        lanes = pl.ds(pl.multiple_of(step * chunk, chunk), chunk)
        arrive(0, out_a, in_a, ahead, start)
        spots = split_bricks(in_a, start)
        answers = []
        for b in range(bricks):
            for orient in range(orients):
                near_a = jnp.maximum(
                    0.0, 1.0 - jnp.abs(spots[b][2 * orient : 2 * orient + 1] - lines)
                )
                near_b = jnp.maximum(
                    0.0, 1.0 - jnp.abs(spots[b][2 * orient + 1 : 2 * orient + 2] - lines)
                )
                weights = near_a[:, None, :] * near_b[None, :, :]
                corner[b, pl.ds(orient * cells, cells), lanes] = weights.reshape(
                    cells, chunk
                ).astype(BF16)
            mixed = matmul(planes_t[b], corner[b, :, lanes], ((1,), (0,))).astype(BF16)
            feature[b, :, lanes] = mixed
            before = matmul(first_t[b], mixed, ((1,), (0,)))
            active = jnp.maximum(before, 0.0).astype(BF16)
            hidden[b, :, lanes] = active
            raw = matmul(last_wide[b].astype(BF16), active, ((1,), (0,)))
            gate = jax.nn.sigmoid(raw)
            soft = jnp.maximum(raw, 0.0) + jnp.log1p(jnp.exp(-jnp.abs(raw)))
            answers.append(jnp.where(chunk_row == 0, soft, gate))
            slope[b, :, lanes] = jnp.where(chunk_row == 0, gate, gate * (1.0 - gate))
        for pair in range(GROUP // 2):
            cut = slice(pair * LANES, (pair + 1) * LANES)
            even, odd = pair_merge(answers[0][:, cut], answers[1][:, cut], low_lanes)
            out_b[start + 2 * pair] = even
            out_b[start + 2 * pair + 1] = odd

        def send_b(offset, inner):
            transfer(1, out_b, in_b, offset, behind(offset)).start()
            return inner

        lax.fori_loop(jnp.maximum(start, 1), start + GROUP, send_b, 0)
        return carry

    lax.fori_loop(0, chunks, forward, 0)
    in_b[0] = out_b[0]

    def wait_b(offset, carry):
        transfer(1, out_b, in_b, offset, behind(offset)).wait_recv()
        return carry

    lax.fori_loop(1, count, wait_b, 0)

    found = jnp.zeros((count * ROWS, total), F32)
    for part in exact_parts(in_b[...].reshape(count * ROWS, LANES)):
        found = found + matmul(part.astype(BF16), lane_hot, ((1,), (0,)))
    found = jnp.sum(
        jnp.where(chosen, found.reshape(count, ROWS, total), 0.0), axis=0
    )
    views = [found[:, i * rays : (i + 1) * rays] for i in range(points)]
    lengths = [
        step_ref[k, pl.ds(s, 1), :] for k in range(crossed) for s in range(samples)
    ]
    running = jnp.zeros((1, rays), F32)
    colour = jnp.zeros((ROWS, rays), F32)
    weights, passed = [], []
    for i in range(points):
        depth = views[i][0:1] * lengths[i]
        weight = jnp.exp(-running) * (1.0 - jnp.exp(-depth))
        running = running + depth
        passed.append(jnp.exp(-running))
        weights.append(weight)
        colour = colour + weight * views[i]
    colour_ref[...] = colour[1:4]
    residual = jnp.where((row >= 1) & (row <= 3), colour - target_tile[...], 0.0)
    behind_sum = jnp.zeros((1, rays), F32)
    cotangents = [None] * points
    for i in reversed(range(points)):
        shade_dot = jnp.sum(views[i] * residual, axis=0, keepdims=True)
        density_cot = (passed[i] * shade_dot - behind_sum) * lengths[i]
        behind_sum = behind_sum + weights[i] * shade_dot
        cotangents[i] = jnp.where(row == 0, density_cot, weights[i] * residual)
    tiles = scatter(jnp.concatenate(cotangents, axis=1))
    out_c[...] = tiles
    in_c[0] = tiles[0]

    def send_c(offset, carry):
        transfer(2, out_c, in_c, offset, ahead(offset)).start()
        return carry

    lax.fori_loop(1, count, send_c, 0)

    plane_grad_ref[...] = jnp.zeros_like(plane_grad_ref)
    first_grad_ref[...] = jnp.zeros_like(first_grad_ref)
    last_total[...] = jnp.zeros_like(last_total)

    def backward(step, carry):
        start = step * GROUP
        lanes = pl.ds(pl.multiple_of(step * chunk, chunk), chunk)
        arrive(2, out_c, in_c, ahead, start)
        pulls = split_bricks(in_c, start)
        for b in range(bricks):
            raw_cot = (pulls[b] * slope[b, :, lanes]).astype(BF16)
            active = hidden[b, :, lanes]
            last_total[b] += matmul(raw_cot, active, ((1,), (1,)))
            pull = matmul(last_wide[b].astype(BF16), raw_cot, ((0,), (0,)))
            before_cot = jnp.where(active.astype(F32) > 0.0, pull, 0.0).astype(BF16)
            first_grad_ref[b] += matmul(feature[b, :, lanes], before_cot, ((1,), (1,)))
            feature_cot = matmul(first_ref[b], before_cot, ((1,), (0,))).astype(BF16)
            for orient in range(orients):
                plane_grad_ref[b, orient] += matmul(
                    corner[b, pl.ds(orient * cells, cells), lanes], feature_cot, ((1,), (1,))
                )
        return carry

    lax.fori_loop(0, chunks, backward, 0)
    for b in range(bricks):
        last_grad_ref[b] = last_total[b, pl.ds(0, 4), :]

    def drain(offset, carry):
        transfer(0, out_a, in_a, offset, ahead(offset)).wait_send()
        transfer(1, out_b, in_b, offset, behind(offset)).wait_send()
        transfer(2, out_c, in_c, offset, ahead(offset)).wait_send()
        return carry

    lax.fori_loop(1, count, drain, 0)


def on_device(
    along_x, along_y,
    brick_ids, cell_index, cell_frac, step_length, target, planes, first_layer, last_layer,
):
    count = along_x * along_y
    bricks, orients, cells, channels = planes.shape
    units = first_layer.shape[2]
    rays, crossed = brick_ids.shape
    samples = step_length.shape[1]
    all_bricks = bricks * count
    capacity = max(2, (3 * rays * crossed + all_bricks - 1) // all_bricks)
    half = LANES // bricks
    assert bricks == 2 and capacity * samples <= half and count % GROUP == 0
    slots = count * half
    total = crossed * samples * rays
    vmem = pl.BlockSpec(memory_space=pltpu.VMEM)
    tile = pltpu.VMEM((count, ROWS, LANES), F32)
    return pl.pallas_call(
        functools.partial(step_kernel, along_x, along_y, capacity),
        out_shape=(
            jax.ShapeDtypeStruct(target.shape, F32),
            jax.ShapeDtypeStruct(planes.shape, F32),
            jax.ShapeDtypeStruct(first_layer.shape, F32),
            jax.ShapeDtypeStruct(last_layer.shape, F32),
        ),
        in_specs=[vmem] * 8,
        out_specs=(vmem,) * 4,
        scratch_shapes=[
            pltpu.VMEM((ROWS, total), F32),
            pltpu.VMEM((ROWS, rays), F32),
            pltpu.VMEM((bricks, ROWS, units), F32),
            tile, tile, tile, tile, tile, tile,
            pltpu.VMEM((bricks, channels, orients * cells), BF16),
            pltpu.VMEM((bricks, units, channels), BF16),
            pltpu.VMEM((bricks, orients * cells, slots), BF16),
            pltpu.VMEM((bricks, channels, slots), BF16),
            pltpu.VMEM((bricks, units, slots), BF16),
            pltpu.VMEM((bricks, ROWS, slots), F32),
            pltpu.VMEM((bricks, ROWS, units), F32),
            pltpu.SemaphoreType.DMA((3, count)),
            pltpu.SemaphoreType.DMA((3, count)),
        ],
        compiler_params=pltpu.CompilerParams(
            collective_id=0, has_side_effects=True, vmem_limit_bytes=56 * 1024 * 1024
        ),
    )(brick_ids.T, cell_index, cell_frac, step_length, target, planes, first_layer, last_layer)


def solution(mesh):
    along_x, along_y = mesh.shape["bx"], mesh.shape["by"]
    return jax.shard_map(
        functools.partial(on_device, along_x, along_y),
        mesh=mesh,
        in_specs=(
            P(("bx", "by"), None),
            P(None, None, None, ("bx", "by")),
            P(None, None, None, ("bx", "by")),
            P(None, None, ("bx", "by")),
            P(None, ("bx", "by")),
            P(("bx", "by"), None, None, None),
            P(("bx", "by"), None, None),
            P(("bx", "by"), None, None),
        ),
        out_specs=(
            P(None, ("bx", "by")),
            P(("bx", "by"), None, None, None),
            P(("bx", "by"), None, None),
            P(("bx", "by"), None, None),
        ),
        check_vma=False,
    )
```

profile of v0, /device:TPU:0, one launch (start us, length us, event | category | flops | bytes accessed | tf_op | source)
XLA Modules:
  0.0 39.3 jit_solution(14079085186514402881)
XLA Ops:
  0.6 34.0 %shard_map.111 = (f32[3,128]{1,0:T(4,128)}, f32[2,3,256,128]{3,2,1,0:T(8,128)}, f32[2,128,256]{2,1,0:T(8,128)}, f32[2,4,256]{2,1,0:T(4,128)}) custom-call(s32[3,128]{1,0:T(4,128)} %bitcast.1, s32[6,3,3,128]{3,2,1,0:T(4,128)} %cell_ref.1, f32[6,3,3,128]{3,2,1,0:T(4,128)} %frac_ref.1, f32[3,3,128]{2,1,0:T(4,128)} %step_ref.1, f32[3,128]{1,0:T(4,128)} %target_ref.1, ...), custom_call_target="tpu_custom_call" | custom-call | tf_op jit(solution)/shard_map/pallas_call | solution.py:317
  34.6 0.0 copy-start.2
  34.6 0.7 %copy-done.2 = f32[3,128]{1,0:T(4,128)S(1)} copy-done((f32[3,128]{1,0:T(4,128)S(1)}, f32[3,128]{1,0:T(4,128)}, u32[]{:S(2)}) %copy-start.2) | copy-done | bytes 1560
  35.3 0.6 %copy.16 = f32[3,128]{1,0:T(4,128)} copy(f32[3,128]{1,0:T(4,128)S(1)} %copy-done.2) | data formatting | bytes 3072
  35.9 0.0 copy-start
  35.9 2.1 %copy.17 = f32[2,3,256,128]{3,2,1,0:T(8,128)} copy(f32[2,3,256,128]{3,2,1,0:T(8,128)} %get-tuple-element.9) | data formatting | bytes 1572864
  38.0 0.0 copy-done
  38.0 0.0 copy-start.1
  38.0 0.7 %copy.18 = f32[2,128,256]{2,1,0:T(8,128)} copy(f32[2,128,256]{2,1,0:T(8,128)S(1)} %copy-done) | data formatting | bytes 524288
  38.7 0.0 copy-done.1
  38.7 0.6 %copy.19 = f32[2,4,256]{2,1,0:T(4,128)} copy(f32[2,4,256]{2,1,0:T(4,128)S(1)} %copy-done.1) | data formatting | bytes 16384
Async XLA Ops:
  34.6 0.7 %copy-start.2 = (f32[3,128]{1,0:T(4,128)S(1)}, f32[3,128]{1,0:T(4,128)}, u32[]{:S(2)}) copy-start(f32[3,128]{1,0:T(4,128)} %get-tuple-element.8) | copy-start | bytes 4612
  35.9 2.1 %copy-start = (f32[2,128,256]{2,1,0:T(8,128)S(1)}, f32[2,128,256]{2,1,0:T(8,128)}, u32[]{:S(2)}) copy-start(f32[2,128,256]{2,1,0:T(8,128)} %get-tuple-element.10) | copy-start | bytes 786436
  38.0 0.7 %copy-start.1 = (f32[2,4,256]{2,1,0:T(4,128)S(1)}, f32[2,4,256]{2,1,0:T(4,128)}, u32[]{:S(2)}) copy-start(f32[2,4,256]{2,1,0:T(4,128)} %get-tuple-element.11) | copy-start | bytes 24580
where the time goes:
time: 39.5 us; the launch traced here: 39.3 us
  Pallas kernels  34 us (86%)
  local copies, waits for them, and re-layouts  4.67 us (12%)
  between operations  0.65 us (2%)
    pallas_call x1, Pallas kernels, on_device(): pl.pallas_call(functools.partial(step_kernel, along_x, along_y, capacity)...  34 us
    unnamed x10, local copies, waits for them, and re-layouts  4.67 us

commit v1 on v0

--- a/solution.py
+++ b/solution.py
@@ -13,17 +13,20 @@
 LANES = 128
 ROWS = 8
 GROUP = 8
+HALF = 4
 
 
 def matmul(lhs, rhs, contract):
     return lax.dot_general(lhs, rhs, (contract, ((), ())), preferred_element_type=F32)
 
 
-def exact_parts(value):
-    high = value.astype(BF16).astype(F32)
-    rest = value - high
-    middle = rest.astype(BF16).astype(F32)
-    return high, middle, rest - middle
+def parts_of(value, number):
+    parts = []
+    for _ in range(number - 1):
+        part = value.astype(BF16).astype(F32)
+        parts.append(part)
+        value = value - part
+    return parts + [value]
 
 
 def pair_merge(even, odd, low_lanes):
@@ -110,14 +113,28 @@
     lane_hot = jnp.where(
         lax.broadcasted_iota(jnp.int32, (LANES, total), 0) == place_all, 1.0, 0.0
     ).astype(BF16)
-    chosen = lax.broadcasted_iota(jnp.int32, (count, ROWS, total), 0) == away_all[None]
-
-    def scatter(value):
-        tiles = jnp.zeros((count * ROWS, LANES), F32)
-        for part in exact_parts(value):
-            spread = jnp.where(chosen, part[None], 0.0).reshape(count * ROWS, total).astype(BF16)
-            tiles = tiles + matmul(spread, lane_hot, ((1,), (1,)))
-        return tiles.reshape(count, ROWS, LANES)
+    whole = lax.broadcasted_iota(jnp.int32, (count, ROWS, total), 0) == away_all[None]
+    halves_of = (count // 2, ROWS, total)
+    paired = (
+        2 * lax.broadcasted_iota(jnp.int32, halves_of, 0)
+        + lax.shift_right_logical(lax.broadcasted_iota(jnp.int32, halves_of, 1), 2)
+    ) == away_all[None]
+
+    def scatter(value, chosen, number):
+        tiles = chosen.shape[0]
+        height = tiles * ROWS
+        spread = jnp.concatenate(
+            [
+                jnp.where(chosen, part[None], 0.0).reshape(height, total).astype(BF16)
+                for part in parts_of(value, number)
+            ],
+            axis=0,
+        )
+        placed = matmul(spread, lane_hot, ((1,), (1,)))
+        merged = placed[:height]
+        for at in range(1, number):
+            merged = merged + placed[at * height : (at + 1) * height]
+        return merged.reshape(tiles, ROWS, LANES)
 
     payload[...] = jnp.zeros_like(payload)
     for k in range(crossed):
@@ -128,7 +145,7 @@
                     cell_ref[axis, k, pl.ds(s, 1), :].astype(F32)
                     + frac_ref[axis, k, pl.ds(s, 1), :]
                 )
-    tiles = scatter(payload[...])
+    tiles = scatter(payload[...], whole, 3)
     out_a[...] = tiles
     in_a[0] = tiles[0]
 
@@ -149,6 +166,7 @@
         last_wide[b, pl.ds(0, 4), :] = last_ref[b].astype(F32)
     target_tile[...] = jnp.zeros_like(target_tile)
     target_tile[pl.ds(1, 3), :] = target_ref[...]
+    target_tile[pl.ds(HALF + 1, 3), :] = target_ref[...]
 
     low_lanes = lax.broadcasted_iota(jnp.int32, (ROWS, LANES), 1) < half
     row = lax.broadcasted_iota(jnp.int32, (ROWS, LANES), 0)
@@ -165,9 +183,8 @@
     def split_bricks(landing, start):
         held = [[] for _ in range(bricks)]
         for pair in range(GROUP // 2):
-            merged = pair_merge(
-                landing[start + 2 * pair], landing[start + 2 * pair + 1], low_lanes
-            )
+            even, odd = landing[start + 2 * pair], landing[start + 2 * pair + 1]
+            merged = pair_merge(even, odd, low_lanes[: even.shape[0]])
             for b in range(bricks):
                 held[b].append(merged[b])
         return [jnp.concatenate(part, axis=1) for part in held]
@@ -203,8 +220,8 @@
         for pair in range(GROUP // 2):
             cut = slice(pair * LANES, (pair + 1) * LANES)
             even, odd = pair_merge(answers[0][:, cut], answers[1][:, cut], low_lanes)
-            out_b[start + 2 * pair] = even
-            out_b[start + 2 * pair + 1] = odd
+            out_b[start + 2 * pair] = even[:HALF]
+            out_b[start + 2 * pair + 1] = odd[:HALF]
 
         def send_b(offset, inner):
             transfer(1, out_b, in_b, offset, behind(offset)).start()
@@ -222,12 +239,16 @@
 
     lax.fori_loop(1, count, wait_b, 0)
 
-    found = jnp.zeros((count * ROWS, total), F32)
-    for part in exact_parts(in_b[...].reshape(count * ROWS, LANES)):
-        found = found + matmul(part.astype(BF16), lane_hot, ((1,), (0,)))
-    found = jnp.sum(
-        jnp.where(chosen, found.reshape(count, ROWS, total), 0.0), axis=0
+    held = jnp.concatenate([in_b[t] for t in range(count)], axis=0)
+    found = matmul(
+        jnp.concatenate([part.astype(BF16) for part in parts_of(held, 2)], axis=0),
+        lane_hot,
+        ((1,), (0,)),
     )
+    found = (found[: count * HALF] + found[count * HALF :]).reshape(halves_of)
+    found = jnp.sum(jnp.where(paired, found, 0.0), axis=0)
+    found = found[:HALF] + found[HALF:]
+    found = jnp.concatenate([found, found], axis=0)
     views = [found[:, i * rays : (i + 1) * rays] for i in range(points)]
     lengths = [
         step_ref[k, pl.ds(s, 1), :] for k in range(crossed) for s in range(samples)
@@ -243,17 +264,18 @@
         weights.append(weight)
         colour = colour + weight * views[i]
     colour_ref[...] = colour[1:4]
-    residual = jnp.where((row >= 1) & (row <= 3), colour - target_tile[...], 0.0)
+    residual = jnp.where((row & 3) > 0, colour - target_tile[...], 0.0)
     behind_sum = jnp.zeros((1, rays), F32)
     cotangents = [None] * points
     for i in reversed(range(points)):
-        shade_dot = jnp.sum(views[i] * residual, axis=0, keepdims=True)
+        shade_dot = jnp.sum((views[i] * residual)[:HALF], axis=0, keepdims=True)
         density_cot = (passed[i] * shade_dot - behind_sum) * lengths[i]
         behind_sum = behind_sum + weights[i] * shade_dot
-        cotangents[i] = jnp.where(row == 0, density_cot, weights[i] * residual)
-    tiles = scatter(jnp.concatenate(cotangents, axis=1))
-    out_c[...] = tiles
-    in_c[0] = tiles[0]
+        cotangents[i] = jnp.where((row & 3) == 0, density_cot, weights[i] * residual)
+    tiles = scatter(jnp.concatenate(cotangents, axis=1), paired, 2)
+    for t in range(count):
+        out_c[t] = tiles[t // 2, (t % 2) * HALF : (t % 2 + 1) * HALF]
+    in_c[0] = out_c[0]
 
     def send_c(offset, carry):
         transfer(2, out_c, in_c, offset, ahead(offset)).start()
@@ -271,17 +293,16 @@
         arrive(2, out_c, in_c, ahead, start)
         pulls = split_bricks(in_c, start)
         for b in range(bricks):
-            raw_cot = (pulls[b] * slope[b, :, lanes]).astype(BF16)
+            raw_cot = (
+                jnp.concatenate([pulls[b], jnp.zeros_like(pulls[b])], axis=0) * slope[b, :, lanes]
+            ).astype(BF16)
             active = hidden[b, :, lanes]
             last_total[b] += matmul(raw_cot, active, ((1,), (1,)))
             pull = matmul(last_wide[b].astype(BF16), raw_cot, ((0,), (0,)))
             before_cot = jnp.where(active.astype(F32) > 0.0, pull, 0.0).astype(BF16)
             first_grad_ref[b] += matmul(feature[b, :, lanes], before_cot, ((1,), (1,)))
             feature_cot = matmul(first_ref[b], before_cot, ((1,), (0,))).astype(BF16)
-            for orient in range(orients):
-                plane_grad_ref[b, orient] += matmul(
-                    corner[b, pl.ds(orient * cells, cells), lanes], feature_cot, ((1,), (1,))
-                )
+            plane_grad_ref[b] += matmul(corner[b, :, lanes], feature_cot, ((1,), (1,)))
         return carry
 
     lax.fori_loop(0, chunks, backward, 0)
@@ -295,6 +316,18 @@
         return carry
 
     lax.fori_loop(1, count, drain, 0)
+
+
+def hand_out(*refs):
+    sources, landings, sems = refs[:4], refs[4:8], refs[8]
+    copies = [
+        pltpu.make_async_copy(source, landing, sems.at[at])
+        for at, (source, landing) in enumerate(zip(sources, landings))
+    ]
+    for copy in copies:
+        copy.start()
+    for copy in copies:
+        copy.wait()
 
 
 def on_device(
@@ -314,21 +347,19 @@
     total = crossed * samples * rays
     vmem = pl.BlockSpec(memory_space=pltpu.VMEM)
     tile = pltpu.VMEM((count, ROWS, LANES), F32)
-    return pl.pallas_call(
+    half_tile = pltpu.VMEM((count, HALF, LANES), F32)
+    flat = (bricks, orients * cells, channels)
+    shapes = (target.shape, flat, first_layer.shape, last_layer.shape)
+    results = pl.pallas_call(
         functools.partial(step_kernel, along_x, along_y, capacity),
-        out_shape=(
-            jax.ShapeDtypeStruct(target.shape, F32),
-            jax.ShapeDtypeStruct(planes.shape, F32),
-            jax.ShapeDtypeStruct(first_layer.shape, F32),
-            jax.ShapeDtypeStruct(last_layer.shape, F32),
-        ),
+        out_shape=[pltpu.VMEM(shape, F32) for shape in shapes],
         in_specs=[vmem] * 8,
-        out_specs=(vmem,) * 4,
+        out_specs=[vmem] * 4,
         scratch_shapes=[
             pltpu.VMEM((ROWS, total), F32),
             pltpu.VMEM((ROWS, rays), F32),
             pltpu.VMEM((bricks, ROWS, units), F32),
-            tile, tile, tile, tile, tile, tile,
+            tile, tile, half_tile, half_tile, half_tile, half_tile,
             pltpu.VMEM((bricks, channels, orients * cells), BF16),
             pltpu.VMEM((bricks, units, channels), BF16),
             pltpu.VMEM((bricks, orients * cells, slots), BF16),
@@ -340,9 +371,17 @@
             pltpu.SemaphoreType.DMA((3, count)),
         ],
         compiler_params=pltpu.CompilerParams(
-            collective_id=0, has_side_effects=True, vmem_limit_bytes=56 * 1024 * 1024
+            collective_id=0, has_side_effects=True, vmem_limit_bytes=48 * 1024 * 1024
         ),
     )(brick_ids.T, cell_index, cell_frac, step_length, target, planes, first_layer, last_layer)
+    colour, plane_grad, first_grad, last_grad = pl.pallas_call(
+        hand_out,
+        out_shape=[jax.ShapeDtypeStruct(shape, F32) for shape in shapes],
+        in_specs=[vmem] * 4,
+        out_specs=[pl.BlockSpec(memory_space=pl.ANY)] * 4,
+        scratch_shapes=[pltpu.SemaphoreType.DMA((4,))],
+    )(*results)
+    return colour, plane_grad.reshape(planes.shape), first_grad, last_grad
 
 
 def solution(mesh):

time: 39.5 us -> 43.2 us (1.094)
  local copies, waits for them, and re-layouts: 4.67 us -> 8.95 us
  Pallas kernels: 34 us -> 33.2 us
    unnamed x10 -> x24, local copies, waits for them, and re-layouts: 4.67 us -> 8.95 us
    pallas_call x1, Pallas kernels: 34 us -> 31 us  [on_device(): pl.pallas_call(functools.partial(step_kernel, along_x, along_y, capacity)...]
    pallas_call x0 -> x1, Pallas kernels: none -> 2.19 us  [on_device(): pl.pallas_call(hand_out, out_shape=[jax.ShapeDtypeStruct(shape, F32) for...]
where the time goes in v1:
time: 43.2 us; the launch traced here: 42.8 us
  Pallas kernels  33.2 us (77%)
  local copies, waits for them, and re-layouts  8.95 us (21%)
  between operations  0.67 us (2%)
    pallas_call x1, Pallas kernels, on_device(): pl.pallas_call(functools.partial(step_kernel, along_x, along_y, capacity)...  31 us
    unnamed x24, local copies, waits for them, and re-layouts  8.95 us
    pallas_call x1, Pallas kernels, on_device(): pl.pallas_call(hand_out, out_shape=[jax.ShapeDtypeStruct(shape, F32) for...  2.19 us

profile of v1, /device:TPU:0, one launch (start us, length us, event | category | flops | bytes accessed | tf_op | source)
XLA Modules:
  0.0 42.8 jit_solution(15760739080539152628)
XLA Ops:
  0.6 0.0 copy-start.1
  0.6 1.0 %copy-done.1 = bf16[2,3,256,128]{3,2,1,0:T(8,128)(2,1)S(1)} copy-done((bf16[2,3,256,128]{3,2,1,0:T(8,128)(2,1)S(1)}, bf16[2,3,256,128]{3,2,1,0:T(8,128)(2,1)}, u32[]{:S(2)}) %copy-start.1) | copy-done | bytes 393240
  1.6 0.0 copy-start.3
  1.6 0.9 %copy-done.3 = bf16[2,128,256]{2,1,0:T(8,128)(2,1)S(1)} copy-done((bf16[2,128,256]{2,1,0:T(8,128)(2,1)S(1)}, bf16[2,128,256]{2,1,0:T(8,128)(2,1)}, u32[]{:S(2)}) %copy-start.3) | copy-done | bytes 131096
  2.5 0.0 copy-start.4
  2.5 0.8 %copy-done.4 = s32[6,3,3,128]{3,2,1,0:T(4,128)S(1)} copy-done((s32[6,3,3,128]{3,2,1,0:T(4,128)S(1)}, s32[6,3,3,128]{3,2,1,0:T(4,128)}, u32[]{:S(2)}) %copy-start.4) | copy-done | bytes 27672
  3.3 0.0 copy-start.5
  3.3 0.8 %copy-done.5 = f32[6,3,3,128]{3,2,1,0:T(4,128)S(1)} copy-done((f32[6,3,3,128]{3,2,1,0:T(4,128)S(1)}, f32[6,3,3,128]{3,2,1,0:T(4,128)}, u32[]{:S(2)}) %copy-start.5) | copy-done | bytes 27672
  4.1 0.0 copy-start.7
  4.1 0.7 %copy-done.7 = f32[3,3,128]{2,1,0:T(4,128)S(1)} copy-done((f32[3,3,128]{2,1,0:T(4,128)S(1)}, f32[3,3,128]{2,1,0:T(4,128)}, u32[]{:S(2)}) %copy-start.7) | copy-done | bytes 4632
  4.8 0.0 copy-start.8
  4.8 0.7 %copy-done.8 = bf16[2,4,256]{2,1,0:T(4,128)(2,1)S(1)} copy-done((bf16[2,4,256]{2,1,0:T(4,128)(2,1)S(1)}, bf16[2,4,256]{2,1,0:T(4,128)(2,1)}, u32[]{:S(2)}) %copy-start.8) | copy-done | bytes 4120
  5.5 0.0 copy-start.9
  5.5 0.7 %copy-done.9 = s32[128,3]{0,1:T(4,128)S(1)} copy-done((s32[128,3]{0,1:T(4,128)S(1)}, s32[128,3]{0,1:T(4,128)}, u32[]{:S(2)}) %copy-start.9) | copy-done | bytes 1560
  6.1 0.0 copy-start.10
  6.1 0.7 %copy-done.10 = f32[3,128]{1,0:T(4,128)S(1)} copy-done((f32[3,128]{1,0:T(4,128)S(1)}, f32[3,128]{1,0:T(4,128)}, u32[]{:S(2)}) %copy-start.10) | copy-done | bytes 1560
  6.8 31.0 %shard_map.111 = (f32[3,128]{1,0:T(4,128)S(1)}, f32[2,768,128]{2,1,0:T(8,128)S(1)}, f32[2,128,256]{2,1,0:T(8,128)S(1)}, f32[2,4,256]{2,1,0:T(4,128)S(1)}) custom-call(s32[3,128]{1,0:T(4,128)S(1)} %bitcast.2, s32[6,3,3,128]{3,2,1,0:T(4,128)S(1)} %copy-done.4, f32[6,3,3,128]{3,2,1,0:T(4,128)S(1)} %copy-done.5, f32[3,3,128]{2,1,0:T(4,128)S(1)} %copy-done.7, ...), custom_call_target="tpu_custom_call" | custom-call | tf_op jit(solution)/shard_map/pallas_call | solution.py:353
  37.8 0.0 copy-start
  37.8 0.9 %copy-done = f32[2,768,128]{2,1,0:T(8,128)} copy-done((f32[2,768,128]{2,1,0:T(8,128)}, f32[2,768,128]{2,1,0:T(8,128)S(1)}, u32[]{:S(2)}) %copy-start) | copy-done | bytes 786456
  38.7 0.0 copy-start.2
  38.7 0.7 %copy-done.2 = f32[2,128,256]{2,1,0:T(8,128)} copy-done((f32[2,128,256]{2,1,0:T(8,128)}, f32[2,128,256]{2,1,0:T(8,128)S(1)}, u32[]{:S(2)}) %copy-start.2) | copy-done | bytes 262168
  39.4 0.0 copy-start.6
  39.4 0.6 %copy-done.6 = f32[2,4,256]{2,1,0:T(4,128)} copy-done((f32[2,4,256]{2,1,0:T(4,128)}, f32[2,4,256]{2,1,0:T(4,128)S(1)}, u32[]{:S(2)}) %copy-start.6) | copy-done | bytes 8216
  40.0 0.0 copy-start.11
  40.0 0.6 %copy-done.11 = f32[3,128]{1,0:T(4,128)} copy-done((f32[3,128]{1,0:T(4,128)}, f32[3,128]{1,0:T(4,128)S(1)}, u32[]{:S(2)}) %copy-start.11) | copy-done | bytes 1560
  40.6 2.2 %shard_map.112 = (f32[3,128]{1,0:T(4,128)}, f32[2,768,128]{2,1,0:T(8,128)}, f32[2,128,256]{2,1,0:T(8,128)}, f32[2,4,256]{2,1,0:T(4,128)}) custom-call(f32[3,128]{1,0:T(4,128)} %copy-done.11, f32[2,768,128]{2,1,0:T(8,128)} %copy-done, f32[2,128,256]{2,1,0:T(8,128)} %copy-done.2, f32[2,4,256]{2,1,0:T(4,128)} %copy-done.6), custom_call_target="tpu_custom_call" | custom-call | tf_op jit(solution)/shard_map/pallas_call | solution.py:377
Async XLA Ops:
  0.6 1.0 %copy-start.1 = (bf16[2,3,256,128]{3,2,1,0:T(8,128)(2,1)S(1)}, bf16[2,3,256,128]{3,2,1,0:T(8,128)(2,1)}, u32[]{:S(2)}) copy-start(bf16[2,3,256,128]{3,2,1,0:T(8,128)(2,1)} %planes_ref.1) | copy-start | bytes 1179652
  1.6 0.9 %copy-start.3 = (bf16[2,128,256]{2,1,0:T(8,128)(2,1)S(1)}, bf16[2,128,256]{2,1,0:T(8,128)(2,1)}, u32[]{:S(2)}) copy-start(bf16[2,128,256]{2,1,0:T(8,128)(2,1)} %first_ref.1) | copy-start | bytes 393220
  2.5 0.8 %copy-start.4 = (s32[6,3,3,128]{3,2,1,0:T(4,128)S(1)}, s32[6,3,3,128]{3,2,1,0:T(4,128)}, u32[]{:S(2)}) copy-start(s32[6,3,3,128]{3,2,1,0:T(4,128)} %cell_ref.1) | copy-start | bytes 82948
  3.3 0.8 %copy-start.5 = (f32[6,3,3,128]{3,2,1,0:T(4,128)S(1)}, f32[6,3,3,128]{3,2,1,0:T(4,128)}, u32[]{:S(2)}) copy-start(f32[6,3,3,128]{3,2,1,0:T(4,128)} %frac_ref.1) | copy-start | bytes 82948
  4.1 0.7 %copy-start.7 = (f32[3,3,128]{2,1,0:T(4,128)S(1)}, f32[3,3,128]{2,1,0:T(4,128)}, u32[]{:S(2)}) copy-start(f32[3,3,128]{2,1,0:T(4,128)} %step_ref.1) | copy-start | bytes 13828
  4.8 0.7 %copy-start.8 = (bf16[2,4,256]{2,1,0:T(4,128)(2,1)S(1)}, bf16[2,4,256]{2,1,0:T(4,128)(2,1)}, u32[]{:S(2)}) copy-start(bf16[2,4,256]{2,1,0:T(4,128)(2,1)} %last_ref.1) | copy-start | bytes 12292
  5.5 0.7 %copy-start.9 = (s32[128,3]{0,1:T(4,128)S(1)}, s32[128,3]{0,1:T(4,128)}, u32[]{:S(2)}) copy-start(s32[128,3]{0,1:T(4,128)} %param.8) | copy-start | bytes 4612
  6.1 0.7 %copy-start.10 = (f32[3,128]{1,0:T(4,128)S(1)}, f32[3,128]{1,0:T(4,128)}, u32[]{:S(2)}) copy-start(f32[3,128]{1,0:T(4,128)} %target_ref.1) | copy-start | bytes 4612
  37.8 0.9 %copy-start = (f32[2,768,128]{2,1,0:T(8,128)}, f32[2,768,128]{2,1,0:T(8,128)S(1)}, u32[]{:S(2)}) copy-start(f32[2,768,128]{2,1,0:T(8,128)S(1)} %get-tuple-element.13.refs_1_) | copy-start | bytes 2359300
  38.7 0.7 %copy-start.2 = (f32[2,128,256]{2,1,0:T(8,128)}, f32[2,128,256]{2,1,0:T(8,128)S(1)}, u32[]{:S(2)}) copy-start(f32[2,128,256]{2,1,0:T(8,128)S(1)} %get-tuple-element.14.refs_2_) | copy-start | bytes 786436
  39.4 0.6 %copy-start.6 = (f32[2,4,256]{2,1,0:T(4,128)}, f32[2,4,256]{2,1,0:T(4,128)S(1)}, u32[]{:S(2)}) copy-start(f32[2,4,256]{2,1,0:T(4,128)S(1)} %get-tuple-element.15.refs_3_) | copy-start | bytes 24580
  40.0 0.6 %copy-start.11 = (f32[3,128]{1,0:T(4,128)}, f32[3,128]{1,0:T(4,128)S(1)}, u32[]{:S(2)}) copy-start(f32[3,128]{1,0:T(4,128)S(1)} %get-tuple-element.12.refs_0_) | copy-start | bytes 4612

commit v2 on v1

--- a/solution.py
+++ b/solution.py
@@ -12,7 +12,7 @@
 BF16 = jnp.bfloat16
 LANES = 128
 ROWS = 8
-GROUP = 8
+CHUNK = 256
 HALF = 4
 
 
@@ -29,21 +29,14 @@
     return parts + [value]
 
 
-def pair_merge(even, odd, low_lanes):
-    half = LANES // 2
-    first = jnp.where(low_lanes, even, pltpu.roll(odd, half, 1))
-    second = jnp.where(low_lanes, pltpu.roll(even, half, 1), odd)
-    return first, second
-
-
 def step_kernel(
     along_x, along_y, capacity,
-    ids_ref, cell_ref, frac_ref, step_ref, target_ref, planes_ref, first_ref, last_ref,
-    colour_ref, plane_grad_ref, first_grad_ref, last_grad_ref,
-    payload, target_tile, last_wide,
+    ids_ref, cell_ref, frac_ref, step_ref, target_ref, last_ref, planes_hbm, first_hbm,
+    colour_ref, corner, feature, hidden, raw_cot, first_ref, last_wide,
+    payload, target_tile, planes_ref, slope,
     out_a, in_a, out_b, in_b, out_c, in_c,
-    planes_t, first_t, corner, feature, hidden, slope, last_total,
-    send_sem, recv_sem,
+    planes_t, first_t,
+    load_sem, send_sem, recv_sem,
 ):
     count = along_x * along_y
     bricks, orients, cells, channels = planes_ref.shape
@@ -54,11 +47,15 @@
     points = crossed * samples
     total = points * rays
     segments = crossed * rays
-    half = LANES // bricks
+    width = capacity * samples
+    slots = corner.shape[2]
     all_bricks = bricks * count
-    chunk = GROUP * half
-    chunks = count // GROUP
     me = lax.axis_index("bx") * along_y + lax.axis_index("by")
+
+    load_planes = pltpu.make_async_copy(planes_hbm, planes_ref, load_sem.at[0])
+    load_first = pltpu.make_async_copy(first_hbm, first_ref, load_sem.at[1])
+    load_planes.start()
+    load_first.start()
 
     def device(number):
         return (lax.div(number, along_y), lax.rem(number, along_y))
@@ -101,7 +98,7 @@
     shift = bricks.bit_length() - 1
     away = lax.shift_right_logical(ids_row, shift) - me
     away = jnp.where(away < 0, away + count, away)
-    place = (ids_row & (bricks - 1)) * half + ranking
+    place = (ids_row & (bricks - 1)) * width + ranking
     away_all, place_all = [], []
     for k in range(crossed):
         block = slice(k * rays, (k + 1) * rays)
@@ -157,55 +154,87 @@
 
     lax.fori_loop(1, count, send_a, 0)
 
+    load_planes.wait()
+    load_first.wait()
     for b in range(bricks):
         for orient in range(orients):
             planes_t[b, :, pl.ds(orient * cells, cells)] = planes_ref[b, orient].T
         first_t[b] = first_ref[b].T
     last_wide[...] = jnp.zeros_like(last_wide)
     for b in range(bricks):
-        last_wide[b, pl.ds(0, 4), :] = last_ref[b].astype(F32)
+        last_wide[b, pl.ds(0, HALF), :] = last_ref[b].astype(F32)
     target_tile[...] = jnp.zeros_like(target_tile)
     target_tile[pl.ds(1, 3), :] = target_ref[...]
     target_tile[pl.ds(HALF + 1, 3), :] = target_ref[...]
 
-    low_lanes = lax.broadcasted_iota(jnp.int32, (ROWS, LANES), 1) < half
     row = lax.broadcasted_iota(jnp.int32, (ROWS, LANES), 0)
-    lines = lax.broadcasted_iota(jnp.int32, (side, chunk), 0).astype(F32)
-    chunk_row = lax.broadcasted_iota(jnp.int32, (ROWS, chunk), 0)
-
-    def arrive(phase, source, landing, peer, start):
-        def wait(offset, carry):
-            transfer(phase, source, landing, offset, peer(offset)).wait_recv()
-            return carry
-
-        lax.fori_loop(jnp.maximum(start, 1), start + GROUP, wait, 0)
-
-    def split_bricks(landing, start):
-        held = [[] for _ in range(bricks)]
-        for pair in range(GROUP // 2):
-            even, odd = landing[start + 2 * pair], landing[start + 2 * pair + 1]
-            merged = pair_merge(even, odd, low_lanes[: even.shape[0]])
-            for b in range(bricks):
-                held[b].append(merged[b])
-        return [jnp.concatenate(part, axis=1) for part in held]
-
-    def forward(step, carry):
-        start = step * GROUP
-        lanes = pl.ds(pl.multiple_of(step * chunk, chunk), chunk)
-        arrive(0, out_a, in_a, ahead, start)
-        spots = split_bricks(in_a, start)
-        answers = []
+    lane = lax.broadcasted_iota(jnp.int32, (ROWS, LANES), 1)
+    lines = lax.broadcasted_iota(jnp.int32, (side, CHUNK), 0).astype(F32)
+    chunk_row = lax.broadcasted_iota(jnp.int32, (ROWS, CHUNK), 0)
+
+    def moved(tile, amount):
+        return pltpu.roll(tile, amount % LANES, 1) if amount % LANES else tile
+
+    def columns(landing, b, block):
+        height = landing.shape[1]
+        at = lane[:height]
+        value = jnp.zeros((height, LANES), F32)
+        base = block * LANES
+        for t in range(base // width, min(count - 1, (base + LANES - 1) // width) + 1):
+            low = width * t - base
+            value = jnp.where(
+                (at >= low) & (at < low + width),
+                moved(landing[t], width * (t - b)),
+                value,
+            )
+        return value
+
+    def tile_of(blocks, t):
+        value = jnp.zeros((ROWS, LANES), F32)
+        base = width * t
         for b in range(bricks):
+            for block in range(base // LANES, (base + width - 1) // LANES + 1):
+                low = max(block * LANES, base) - base + b * width
+                high = min((block + 1) * LANES, base + width) - base + b * width
+                value = jnp.where(
+                    (lane >= low) & (lane < high),
+                    moved(blocks[b][block], width * (b - t)),
+                    value,
+                )
+        return value
+
+    def wait_a(offset, carry):
+        transfer(0, out_a, in_a, offset, ahead(offset)).wait_recv()
+        return carry
+
+    def send_b(offset, carry):
+        transfer(1, out_b, in_b, offset, behind(offset)).start()
+        return carry
+
+    blocks = [[] for _ in range(bricks)]
+    arrived, returned = 1, 0
+    for chunk in range(slots // CHUNK):
+        stop = (chunk + 1) * CHUNK
+        lanes = pl.ds(chunk * CHUNK, CHUNK)
+        needed = min(count, (stop - 1) // width + 1)
+        if needed > arrived:
+            lax.fori_loop(arrived, needed, wait_a, 0)
+            arrived = needed
+        for b in range(bricks):
+            spots = jnp.concatenate(
+                [columns(in_a, b, at) for at in range(chunk * CHUNK // LANES, stop // LANES)],
+                axis=1,
+            )
             for orient in range(orients):
                 near_a = jnp.maximum(
-                    0.0, 1.0 - jnp.abs(spots[b][2 * orient : 2 * orient + 1] - lines)
+                    0.0, 1.0 - jnp.abs(spots[2 * orient : 2 * orient + 1] - lines)
                 )
                 near_b = jnp.maximum(
-                    0.0, 1.0 - jnp.abs(spots[b][2 * orient + 1 : 2 * orient + 2] - lines)
+                    0.0, 1.0 - jnp.abs(spots[2 * orient + 1 : 2 * orient + 2] - lines)
                 )
                 weights = near_a[:, None, :] * near_b[None, :, :]
                 corner[b, pl.ds(orient * cells, cells), lanes] = weights.reshape(
-                    cells, chunk
+                    cells, CHUNK
                 ).astype(BF16)
             mixed = matmul(planes_t[b], corner[b, :, lanes], ((1,), (0,))).astype(BF16)
             feature[b, :, lanes] = mixed
@@ -215,22 +244,16 @@
             raw = matmul(last_wide[b].astype(BF16), active, ((1,), (0,)))
             gate = jax.nn.sigmoid(raw)
             soft = jnp.maximum(raw, 0.0) + jnp.log1p(jnp.exp(-jnp.abs(raw)))
-            answers.append(jnp.where(chunk_row == 0, soft, gate))
+            answer = jnp.where(chunk_row == 0, soft, gate)
             slope[b, :, lanes] = jnp.where(chunk_row == 0, gate, gate * (1.0 - gate))
-        for pair in range(GROUP // 2):
-            cut = slice(pair * LANES, (pair + 1) * LANES)
-            even, odd = pair_merge(answers[0][:, cut], answers[1][:, cut], low_lanes)
-            out_b[start + 2 * pair] = even[:HALF]
-            out_b[start + 2 * pair + 1] = odd[:HALF]
-
-        def send_b(offset, inner):
-            transfer(1, out_b, in_b, offset, behind(offset)).start()
-            return inner
-
-        lax.fori_loop(jnp.maximum(start, 1), start + GROUP, send_b, 0)
-        return carry
-
-    lax.fori_loop(0, chunks, forward, 0)
+            for at in range(CHUNK // LANES):
+                blocks[b].append(answer[:, at * LANES : (at + 1) * LANES])
+        ready = min(count, stop // width)
+        for t in range(returned, ready):
+            out_b[t] = tile_of(blocks, t)[:HALF]
+        if ready > max(returned, 1):
+            lax.fori_loop(max(returned, 1), ready, send_b, 0)
+        returned = max(returned, ready)
     in_b[0] = out_b[0]
 
     def wait_b(offset, carry):
@@ -283,49 +306,51 @@
 
     lax.fori_loop(1, count, send_c, 0)
 
-    plane_grad_ref[...] = jnp.zeros_like(plane_grad_ref)
-    first_grad_ref[...] = jnp.zeros_like(first_grad_ref)
-    last_total[...] = jnp.zeros_like(last_total)
-
-    def backward(step, carry):
-        start = step * GROUP
-        lanes = pl.ds(pl.multiple_of(step * chunk, chunk), chunk)
-        arrive(2, out_c, in_c, ahead, start)
-        pulls = split_bricks(in_c, start)
-        for b in range(bricks):
-            raw_cot = (
-                jnp.concatenate([pulls[b], jnp.zeros_like(pulls[b])], axis=0) * slope[b, :, lanes]
-            ).astype(BF16)
-            active = hidden[b, :, lanes]
-            last_total[b] += matmul(raw_cot, active, ((1,), (1,)))
-            pull = matmul(last_wide[b].astype(BF16), raw_cot, ((0,), (0,)))
-            before_cot = jnp.where(active.astype(F32) > 0.0, pull, 0.0).astype(BF16)
-            first_grad_ref[b] += matmul(feature[b, :, lanes], before_cot, ((1,), (1,)))
-            feature_cot = matmul(first_ref[b], before_cot, ((1,), (0,))).astype(BF16)
-            plane_grad_ref[b] += matmul(corner[b, :, lanes], feature_cot, ((1,), (1,)))
-        return carry
-
-    lax.fori_loop(0, chunks, backward, 0)
-    for b in range(bricks):
-        last_grad_ref[b] = last_total[b, pl.ds(0, 4), :]
-
     def drain(offset, carry):
         transfer(0, out_a, in_a, offset, ahead(offset)).wait_send()
         transfer(1, out_b, in_b, offset, behind(offset)).wait_send()
-        transfer(2, out_c, in_c, offset, ahead(offset)).wait_send()
+        transfer(2, out_c, in_c, offset, ahead(offset)).wait()
         return carry
 
     lax.fori_loop(1, count, drain, 0)
-
-
-def hand_out(*refs):
-    sources, landings, sems = refs[:4], refs[4:8], refs[8]
-    copies = [
-        pltpu.make_async_copy(source, landing, sems.at[at])
-        for at, (source, landing) in enumerate(zip(sources, landings))
-    ]
-    for copy in copies:
-        copy.start()
+    for b in range(bricks):
+        for block in range(slots // LANES):
+            lanes = pl.ds(block * LANES, LANES)
+            pull = columns(in_c, b, block)
+            raw_cot[b, :, lanes] = (
+                jnp.concatenate([pull, jnp.zeros_like(pull)], axis=0) * slope[b, :, lanes]
+            )
+
+
+def gradient_kernel(
+    colour_in, corner, feature, hidden, raw_cot, first_ref, last_wide,
+    colour_out, plane_out, first_out, last_out,
+    plane_part, first_part, last_part, before_cot, feature_cot, sems,
+):
+    bricks, _, slots = corner.shape
+    copies = [pltpu.make_async_copy(colour_in, colour_out, sems.at[0])]
+    copies[0].start()
+    for b in range(bricks):
+        cot = raw_cot[b].astype(BF16)
+        for chunk in range(slots // CHUNK):
+            lanes = pl.ds(chunk * CHUNK, CHUNK)
+            pull = matmul(
+                last_wide[b].astype(BF16),
+                cot[:, chunk * CHUNK : (chunk + 1) * CHUNK],
+                ((0,), (0,)),
+            )
+            masked = jnp.where(hidden[b, :, lanes].astype(F32) > 0.0, pull, 0.0).astype(BF16)
+            before_cot[:, lanes] = masked
+            feature_cot[:, lanes] = matmul(first_ref[b], masked, ((1,), (0,))).astype(BF16)
+        plane_part[b] = matmul(corner[b], feature_cot[...], ((1,), (1,)))
+        first_part[b] = matmul(feature[b], before_cot[...], ((1,), (1,)))
+        last_part[b] = matmul(cot, hidden[b], ((1,), (1,)))[:HALF]
+        for at, (source, landing) in enumerate(
+            ((plane_part, plane_out), (first_part, first_out), (last_part, last_out))
+        ):
+            copy = pltpu.make_async_copy(source.at[b], landing.at[b], sems.at[1 + 3 * b + at])
+            copy.start()
+            copies.append(copy)
     for copy in copies:
         copy.wait()
 
@@ -341,46 +366,66 @@
     samples = step_length.shape[1]
     all_bricks = bricks * count
     capacity = max(2, (3 * rays * crossed + all_bricks - 1) // all_bricks)
-    half = LANES // bricks
-    assert bricks == 2 and capacity * samples <= half and count % GROUP == 0
-    slots = count * half
+    width = capacity * samples
+    assert bricks == 2 and bricks * width <= LANES and count % 2 == 0
+    slots = (count * width + CHUNK - 1) // CHUNK * CHUNK
     total = crossed * samples * rays
+    flat = (bricks, orients * cells, channels)
     vmem = pl.BlockSpec(memory_space=pltpu.VMEM)
+    hbm = pl.BlockSpec(memory_space=pltpu.HBM)
     tile = pltpu.VMEM((count, ROWS, LANES), F32)
     half_tile = pltpu.VMEM((count, HALF, LANES), F32)
-    flat = (bricks, orients * cells, channels)
-    shapes = (target.shape, flat, first_layer.shape, last_layer.shape)
-    results = pl.pallas_call(
+    limit = 32 * 1024 * 1024
+    inputs = (
+        brick_ids.T, cell_index, cell_frac, step_length, target, last_layer, planes, first_layer
+    )
+    held = pl.pallas_call(
         functools.partial(step_kernel, along_x, along_y, capacity),
-        out_shape=[pltpu.VMEM(shape, F32) for shape in shapes],
-        in_specs=[vmem] * 8,
-        out_specs=[vmem] * 4,
-        scratch_shapes=[
-            pltpu.VMEM((ROWS, total), F32),
-            pltpu.VMEM((ROWS, rays), F32),
-            pltpu.VMEM((bricks, ROWS, units), F32),
-            tile, tile, half_tile, half_tile, half_tile, half_tile,
-            pltpu.VMEM((bricks, channels, orients * cells), BF16),
-            pltpu.VMEM((bricks, units, channels), BF16),
+        out_shape=[
+            pltpu.VMEM(target.shape, F32),
             pltpu.VMEM((bricks, orients * cells, slots), BF16),
             pltpu.VMEM((bricks, channels, slots), BF16),
             pltpu.VMEM((bricks, units, slots), BF16),
             pltpu.VMEM((bricks, ROWS, slots), F32),
+            pltpu.VMEM(first_layer.shape, BF16),
             pltpu.VMEM((bricks, ROWS, units), F32),
+        ],
+        in_specs=[vmem] * 6 + [hbm] * 2,
+        out_specs=[vmem] * 7,
+        scratch_shapes=[
+            pltpu.VMEM((ROWS, total), F32),
+            pltpu.VMEM((ROWS, rays), F32),
+            pltpu.VMEM(planes.shape, BF16),
+            pltpu.VMEM((bricks, ROWS, slots), F32),
+            tile, tile, half_tile, half_tile, half_tile, half_tile,
+            pltpu.VMEM((bricks, channels, orients * cells), BF16),
+            pltpu.VMEM((bricks, units, channels), BF16),
+            pltpu.SemaphoreType.DMA((2,)),
             pltpu.SemaphoreType.DMA((3, count)),
             pltpu.SemaphoreType.DMA((3, count)),
         ],
         compiler_params=pltpu.CompilerParams(
-            collective_id=0, has_side_effects=True, vmem_limit_bytes=48 * 1024 * 1024
+            collective_id=0, has_side_effects=True, vmem_limit_bytes=limit
         ),
-    )(brick_ids.T, cell_index, cell_frac, step_length, target, planes, first_layer, last_layer)
+    )(*[pltpu.with_memory_space_constraint(value, pltpu.HBM) for value in inputs])
     colour, plane_grad, first_grad, last_grad = pl.pallas_call(
-        hand_out,
-        out_shape=[jax.ShapeDtypeStruct(shape, F32) for shape in shapes],
-        in_specs=[vmem] * 4,
-        out_specs=[pl.BlockSpec(memory_space=pl.ANY)] * 4,
-        scratch_shapes=[pltpu.SemaphoreType.DMA((4,))],
-    )(*results)
+        gradient_kernel,
+        out_shape=[
+            jax.ShapeDtypeStruct(shape, F32)
+            for shape in (target.shape, flat, first_layer.shape, last_layer.shape)
+        ],
+        in_specs=[vmem] * 7,
+        out_specs=[hbm] * 4,
+        scratch_shapes=[
+            pltpu.VMEM(flat, F32),
+            pltpu.VMEM(first_layer.shape, F32),
+            pltpu.VMEM(last_layer.shape, F32),
+            pltpu.VMEM((units, slots), BF16),
+            pltpu.VMEM((channels, slots), BF16),
+            pltpu.SemaphoreType.DMA((1 + 3 * bricks,)),
+        ],
+        compiler_params=pltpu.CompilerParams(vmem_limit_bytes=limit),
+    )(*[pltpu.with_memory_space_constraint(value, pltpu.VMEM) for value in held])
     return colour, plane_grad.reshape(planes.shape), first_grad, last_grad
 
 

time: 43.2 us -> 35.2 us (0.81)
  local copies, waits for them, and re-layouts: 8.95 us -> 0 us
  Pallas kernels: 33.2 us -> 34.3 us
    unnamed x24 -> x0, local copies, waits for them, and re-layouts: 8.95 us -> none
    pallas_call x1, Pallas kernels: 2.19 us -> 6.02 us  [on_device(): pl.pallas_call(gradient_kernel, out_shape=[jax.ShapeDtypeStruct(shape, F3...]
    pallas_call x1, Pallas kernels: 31 us -> 28.3 us  [on_device(): pl.pallas_call(functools.partial(step_kernel, along_x, along_y, capacity)...]
where the time goes in v2:
time: 35.2 us; the launch traced here: 35 us
  Pallas kernels  34.3 us (97%)
  between operations  0.64 us (2%)
    pallas_call x1, Pallas kernels, on_device(): pl.pallas_call(functools.partial(step_kernel, along_x, along_y, capacity)...  28.3 us
    pallas_call x1, Pallas kernels, on_device(): pl.pallas_call(gradient_kernel, out_shape=[jax.ShapeDtypeStruct(shape, F3...  6.02 us

profile of v2, /device:TPU:0, one launch (start us, length us, event | category | flops | bytes accessed | tf_op | source)
XLA Modules:
  0.0 35.0 jit_solution(11789579859994336779)
XLA Ops:
  0.6 28.3 %shard_map.111 = (f32[3,128]{1,0:T(4,128)S(1)}, bf16[2,768,1792]{2,1,0:T(8,128)(2,1)S(1)}, bf16[2,128,1792]{2,1,0:T(8,128)(2,1)S(1)}, bf16[2,256,1792]{2,1,0:T(8...) custom-call(s32[3,128]{1,0:T(4,128)} %bitcast.2, ...), custom_call_target="tpu_custom_call" | custom-call | tf_op jit(solution)/shard_map/pallas_call | solution.py:382
  29.0 6.0 %shard_map.112 = (f32[3,128]{1,0:T(4,128)}, f32[2,768,128]{2,1,0:T(8,128)}, f32[2,128,256]{2,1,0:T(8,128)}, f32[2,4,256]{2,1,0:T(4,128)}) custom-call(f32[3,128]{1,0:T(4,128)S(1)} %get-tuple-element.15.colour_in, bf16[2,768,1792]{2,1,0:T(8,128)(2,1)S(1)} %get-tuple-element.16.corner, bf16[2,128,1792]{2,1,0:T(8,128)(2,1)S(1)} %get-tuple-element.17.feature, ...), custom_call_target="tpu_custom_call" | custom-call | tf_op jit(solution)/shard_map/pallas_call | solution.py:411

commit v3 on v2

--- a/solution.py
+++ b/solution.py
@@ -33,7 +33,7 @@
     along_x, along_y, capacity,
     ids_ref, cell_ref, frac_ref, step_ref, target_ref, last_ref, planes_hbm, first_hbm,
     colour_ref, corner, feature, hidden, raw_cot, first_ref, last_wide,
-    payload, target_tile, planes_ref, slope,
+    payload, target_tile, planes_ref, spots, answers, slope,
     out_a, in_a, out_b, in_b, out_c, in_c,
     planes_t, first_t,
     load_sem, send_sem, recv_sem,
@@ -57,24 +57,41 @@
     load_planes.start()
     load_first.start()
 
+    shift_y = along_y.bit_length() - 1
+
     def device(number):
-        return (lax.div(number, along_y), lax.rem(number, along_y))
+        number = number & (count - 1)
+        return (lax.shift_right_logical(number, shift_y), number & (along_y - 1))
 
     def ahead(offset):
-        return device(lax.rem(me + offset, count))
+        return device(me + offset)
 
     def behind(offset):
-        return device(lax.rem(me + count - offset, count))
-
-    def transfer(phase, source, landing, offset, peer):
+        return device(me + count - offset)
+
+    def transfer(phase, part, source, landing, where, peer):
         return pltpu.make_async_remote_copy(
-            src_ref=source.at[offset],
-            dst_ref=landing.at[offset],
-            send_sem=send_sem.at[phase, offset],
-            recv_sem=recv_sem.at[phase, offset],
+            src_ref=source.at[where],
+            dst_ref=landing.at[where],
+            send_sem=send_sem.at[phase],
+            recv_sem=recv_sem.at[phase, part],
             device_id=peer,
             device_id_type=MESH,
         )
+
+    def spread_out(phase, part, source, landing, peer, start, stop):
+        def send(offset, carry):
+            transfer(phase, part, source, landing, offset, peer(offset)).start()
+            return carry
+
+        lax.fori_loop(start, stop, send, 0)
+
+    def gather_in(phase, part, source, landing, start, stop):
+        rows = pl.ds(start, stop - start)
+        transfer(phase, part, source, landing, rows, ahead(1)).wait_recv()
+
+    def sent(phase, source, landing):
+        transfer(phase, 0, source, landing, pl.ds(1, count - 1), ahead(1)).wait_send()
 
     barrier = pltpu.get_barrier_semaphore()
 
@@ -143,16 +160,16 @@
                     + frac_ref[axis, k, pl.ds(s, 1), :]
                 )
     tiles = scatter(payload[...], whole, 3)
-    out_a[...] = tiles
-    in_a[0] = tiles[0]
+    out_a[...] = tiles[:, : 2 * orients]
+    in_a[0] = tiles[0, : 2 * orients]
 
     pl.semaphore_wait(barrier, count - 1)
 
-    def send_a(offset, carry):
-        transfer(0, out_a, in_a, offset, ahead(offset)).start()
-        return carry
-
-    lax.fori_loop(1, count, send_a, 0)
+    chunks = slots // CHUNK
+    edges = [0, chunks // 2 * CHUNK, slots]
+    reach = [1] + [min(count, (stop - 1) // width + 1) for stop in edges[1:]]
+    for part in range(2):
+        spread_out(0, part, out_a, in_a, ahead, reach[part], reach[part + 1])
 
     load_planes.wait()
     load_first.wait()
@@ -189,7 +206,7 @@
             )
         return value
 
-    def tile_of(blocks, t):
+    def tile_of(values, t):
         value = jnp.zeros((ROWS, LANES), F32)
         base = width * t
         for b in range(bricks):
@@ -198,39 +215,20 @@
                 high = min((block + 1) * LANES, base + width) - base + b * width
                 value = jnp.where(
                     (lane >= low) & (lane < high),
-                    moved(blocks[b][block], width * (b - t)),
+                    moved(values[b, :, pl.ds(block * LANES, LANES)], width * (b - t)),
                     value,
                 )
         return value
 
-    def wait_a(offset, carry):
-        transfer(0, out_a, in_a, offset, ahead(offset)).wait_recv()
-        return carry
-
-    def send_b(offset, carry):
-        transfer(1, out_b, in_b, offset, behind(offset)).start()
-        return carry
-
-    blocks = [[] for _ in range(bricks)]
-    arrived, returned = 1, 0
-    for chunk in range(slots // CHUNK):
-        stop = (chunk + 1) * CHUNK
-        lanes = pl.ds(chunk * CHUNK, CHUNK)
-        needed = min(count, (stop - 1) // width + 1)
-        if needed > arrived:
-            lax.fori_loop(arrived, needed, wait_a, 0)
-            arrived = needed
+    def forward(chunk, carry):
+        lanes = pl.ds(pl.multiple_of(chunk * CHUNK, CHUNK), CHUNK)
         for b in range(bricks):
-            spots = jnp.concatenate(
-                [columns(in_a, b, at) for at in range(chunk * CHUNK // LANES, stop // LANES)],
-                axis=1,
-            )
             for orient in range(orients):
                 near_a = jnp.maximum(
-                    0.0, 1.0 - jnp.abs(spots[2 * orient : 2 * orient + 1] - lines)
+                    0.0, 1.0 - jnp.abs(spots[b, pl.ds(2 * orient, 1), lanes] - lines)
                 )
                 near_b = jnp.maximum(
-                    0.0, 1.0 - jnp.abs(spots[2 * orient + 1 : 2 * orient + 2] - lines)
+                    0.0, 1.0 - jnp.abs(spots[b, pl.ds(2 * orient + 1, 1), lanes] - lines)
                 )
                 weights = near_a[:, None, :] * near_b[None, :, :]
                 corner[b, pl.ds(orient * cells, cells), lanes] = weights.reshape(
@@ -244,23 +242,27 @@
             raw = matmul(last_wide[b].astype(BF16), active, ((1,), (0,)))
             gate = jax.nn.sigmoid(raw)
             soft = jnp.maximum(raw, 0.0) + jnp.log1p(jnp.exp(-jnp.abs(raw)))
-            answer = jnp.where(chunk_row == 0, soft, gate)
+            answers[b, :, lanes] = jnp.where(chunk_row == 0, soft, gate)
             slope[b, :, lanes] = jnp.where(chunk_row == 0, gate, gate * (1.0 - gate))
-            for at in range(CHUNK // LANES):
-                blocks[b].append(answer[:, at * LANES : (at + 1) * LANES])
-        ready = min(count, stop // width)
+        return carry
+
+    returned = 0
+    for part in range(2):
+        gather_in(0, part, out_a, in_a, reach[part], reach[part + 1])
+        for b in range(bricks):
+            for block in range(edges[part] // LANES, edges[part + 1] // LANES):
+                spots[b, pl.ds(0, 2 * orients), pl.ds(block * LANES, LANES)] = columns(
+                    in_a, b, block
+                )
+        lax.fori_loop(edges[part] // CHUNK, edges[part + 1] // CHUNK, forward, 0)
+        ready = min(count, edges[part + 1] // width)
         for t in range(returned, ready):
-            out_b[t] = tile_of(blocks, t)[:HALF]
-        if ready > max(returned, 1):
-            lax.fori_loop(max(returned, 1), ready, send_b, 0)
-        returned = max(returned, ready)
+            out_b[t] = tile_of(answers, t)[:HALF]
+        spread_out(1, 0, out_b, in_b, behind, max(returned, 1), ready)
+        returned = ready
     in_b[0] = out_b[0]
-
-    def wait_b(offset, carry):
-        transfer(1, out_b, in_b, offset, behind(offset)).wait_recv()
-        return carry
-
-    lax.fori_loop(1, count, wait_b, 0)
+    sent(0, out_a, in_a)
+    gather_in(1, 0, out_b, in_b, 1, count)
 
     held = jnp.concatenate([in_b[t] for t in range(count)], axis=0)
     found = matmul(
@@ -300,19 +302,16 @@
         out_c[t] = tiles[t // 2, (t % 2) * HALF : (t % 2 + 1) * HALF]
     in_c[0] = out_c[0]
 
-    def send_c(offset, carry):
-        transfer(2, out_c, in_c, offset, ahead(offset)).start()
+    def send_c(turn, carry):
+        offset = turn + count // 2 - 1
+        offset = jnp.where(offset >= count, offset - (count - 1), offset)
+        transfer(2, 0, out_c, in_c, offset, ahead(offset)).start()
         return carry
 
     lax.fori_loop(1, count, send_c, 0)
-
-    def drain(offset, carry):
-        transfer(0, out_a, in_a, offset, ahead(offset)).wait_send()
-        transfer(1, out_b, in_b, offset, behind(offset)).wait_send()
-        transfer(2, out_c, in_c, offset, ahead(offset)).wait()
-        return carry
-
-    lax.fori_loop(1, count, drain, 0)
+    sent(1, out_b, in_b)
+    gather_in(2, 0, out_c, in_c, 1, count)
+    sent(2, out_c, in_c)
     for b in range(bricks):
         for block in range(slots // LANES):
             lanes = pl.ds(block * LANES, LANES)
@@ -328,9 +327,17 @@
     plane_part, first_part, last_part, before_cot, feature_cot, sems,
 ):
     bricks, _, slots = corner.shape
-    copies = [pltpu.make_async_copy(colour_in, colour_out, sems.at[0])]
-    copies[0].start()
-    for b in range(bricks):
+    colour_copy = pltpu.make_async_copy(colour_in, colour_out, sems.at[0, 3])
+    colour_copy.start()
+
+    def result_copies(b):
+        pairs = ((plane_part, plane_out), (first_part, first_out), (last_part, last_out))
+        return [
+            pltpu.make_async_copy(source.at[b], landing.at[b], sems.at[b, at])
+            for at, (source, landing) in enumerate(pairs)
+        ]
+
+    def one_brick(b, carry):
         cot = raw_cot[b].astype(BF16)
         for chunk in range(slots // CHUNK):
             lanes = pl.ds(chunk * CHUNK, CHUNK)
@@ -345,14 +352,15 @@
         plane_part[b] = matmul(corner[b], feature_cot[...], ((1,), (1,)))
         first_part[b] = matmul(feature[b], before_cot[...], ((1,), (1,)))
         last_part[b] = matmul(cot, hidden[b], ((1,), (1,)))[:HALF]
-        for at, (source, landing) in enumerate(
-            ((plane_part, plane_out), (first_part, first_out), (last_part, last_out))
-        ):
-            copy = pltpu.make_async_copy(source.at[b], landing.at[b], sems.at[1 + 3 * b + at])
+        for copy in result_copies(b):
             copy.start()
-            copies.append(copy)
-    for copy in copies:
-        copy.wait()
+        return carry
+
+    lax.fori_loop(0, bricks, one_brick, 0)
+    colour_copy.wait()
+    for b in range(bricks):
+        for copy in result_copies(b):
+            copy.wait()
 
 
 def on_device(
@@ -367,13 +375,15 @@
     all_bricks = bricks * count
     capacity = max(2, (3 * rays * crossed + all_bricks - 1) // all_bricks)
     width = capacity * samples
-    assert bricks == 2 and bricks * width <= LANES and count % 2 == 0
+    assert bricks == 2 and bricks * width <= LANES
+    assert count & (count - 1) == 0 and along_y & (along_y - 1) == 0
     slots = (count * width + CHUNK - 1) // CHUNK * CHUNK
     total = crossed * samples * rays
     flat = (bricks, orients * cells, channels)
     vmem = pl.BlockSpec(memory_space=pltpu.VMEM)
     hbm = pl.BlockSpec(memory_space=pltpu.HBM)
-    tile = pltpu.VMEM((count, ROWS, LANES), F32)
+    wide = pltpu.VMEM((bricks, ROWS, slots), F32)
+    tile = pltpu.VMEM((count, 2 * orients, LANES), F32)
     half_tile = pltpu.VMEM((count, HALF, LANES), F32)
     limit = 32 * 1024 * 1024
     inputs = (
@@ -396,13 +406,13 @@
             pltpu.VMEM((ROWS, total), F32),
             pltpu.VMEM((ROWS, rays), F32),
             pltpu.VMEM(planes.shape, BF16),
-            pltpu.VMEM((bricks, ROWS, slots), F32),
+            wide, wide, wide,
             tile, tile, half_tile, half_tile, half_tile, half_tile,
             pltpu.VMEM((bricks, channels, orients * cells), BF16),
             pltpu.VMEM((bricks, units, channels), BF16),
             pltpu.SemaphoreType.DMA((2,)),
-            pltpu.SemaphoreType.DMA((3, count)),
-            pltpu.SemaphoreType.DMA((3, count)),
+            pltpu.SemaphoreType.DMA((3,)),
+            pltpu.SemaphoreType.DMA((3, 2)),
         ],
         compiler_params=pltpu.CompilerParams(
             collective_id=0, has_side_effects=True, vmem_limit_bytes=limit
@@ -422,7 +432,7 @@
             pltpu.VMEM(last_layer.shape, F32),
             pltpu.VMEM((units, slots), BF16),
             pltpu.VMEM((channels, slots), BF16),
-            pltpu.SemaphoreType.DMA((1 + 3 * bricks,)),
+            pltpu.SemaphoreType.DMA((bricks, 4)),
         ],
         compiler_params=pltpu.CompilerParams(vmem_limit_bytes=limit),
     )(*[pltpu.with_memory_space_constraint(value, pltpu.VMEM) for value in held])

time: 35.2 us -> 35.8 us (1.017)
  Pallas kernels: 34.3 us -> 35 us
    pallas_call x1, Pallas kernels: 6.02 us -> 6.43 us  [on_device(): pl.pallas_call(gradient_kernel, out_shape=[jax.ShapeDtypeStruct(shape, F3...]
where the time goes in v3:
time: 35.8 us; the launch traced here: 35.7 us
  Pallas kernels  35 us (98%)
  between operations  0.64 us (2%)
    pallas_call x1, Pallas kernels, on_device(): pl.pallas_call(functools.partial(step_kernel, along_x, along_y, capacity)...  28.6 us
    pallas_call x1, Pallas kernels, on_device(): pl.pallas_call(gradient_kernel, out_shape=[jax.ShapeDtypeStruct(shape, F3...  6.43 us

profile of v3, /device:TPU:0, one launch (start us, length us, event | category | flops | bytes accessed | tf_op | source)
XLA Modules:
  0.0 35.7 jit_solution(2439284563115171040)
XLA Ops:
  0.6 28.6 %shard_map.111 = (f32[3,128]{1,0:T(4,128)S(1)}, bf16[2,768,1792]{2,1,0:T(8,128)(2,1)S(1)}, bf16[2,128,1792]{2,1,0:T(8,128)(2,1)S(1)}, bf16[2,256,1792]{2,1,0:T(8...) custom-call(s32[3,128]{1,0:T(4,128)} %bitcast.2, ...), custom_call_target="tpu_custom_call" | custom-call | tf_op jit(solution)/shard_map/pallas_call | solution.py:392
  29.2 6.4 %shard_map.112 = (f32[3,128]{1,0:T(4,128)}, f32[2,768,128]{2,1,0:T(8,128)}, f32[2,128,256]{2,1,0:T(8,128)}, f32[2,4,256]{2,1,0:T(4,128)}) custom-call(f32[3,128]{1,0:T(4,128)S(1)} %get-tuple-element.15.colour_in, bf16[2,768,1792]{2,1,0:T(8,128)(2,1)S(1)} %get-tuple-element.16.corner, bf16[2,128,1792]{2,1,0:T(8,128)(2,1)S(1)} %get-tuple-element.17.feature, ...), custom_call_target="tpu_custom_call" | custom-call | tf_op jit(solution)/shard_map/pallas_call | solution.py:421

commit v4 on v3

--- a/solution.py
+++ b/solution.py
@@ -84,7 +84,7 @@
             transfer(phase, part, source, landing, offset, peer(offset)).start()
             return carry
 
-        lax.fori_loop(start, stop, send, 0)
+        lax.fori_loop(start, stop, send, 0, unroll=True)
 
     def gather_in(phase, part, source, landing, start, stop):
         rows = pl.ds(start, stop - start)
@@ -127,26 +127,31 @@
     lane_hot = jnp.where(
         lax.broadcasted_iota(jnp.int32, (LANES, total), 0) == place_all, 1.0, 0.0
     ).astype(BF16)
-    whole = lax.broadcasted_iota(jnp.int32, (count, ROWS, total), 0) == away_all[None]
-    halves_of = (count // 2, ROWS, total)
-    paired = (
-        2 * lax.broadcasted_iota(jnp.int32, halves_of, 0)
-        + lax.shift_right_logical(lax.broadcasted_iota(jnp.int32, halves_of, 1), 2)
-    ) == away_all[None]
-
-    def scatter(value, chosen, number):
+    def whole(start, stop):
+        shape = (stop - start, ROWS, total)
+        return lax.broadcasted_iota(jnp.int32, shape, 0) + start == away_all[None]
+
+    def paired(start, stop):
+        shape = ((stop - start) // 2, ROWS, total)
+        return (
+            2 * lax.broadcasted_iota(jnp.int32, shape, 0)
+            + lax.shift_right_logical(lax.broadcasted_iota(jnp.int32, shape, 1), 2)
+            + start
+        ) == away_all[None]
+
+    def scatter(parts, chosen):
         tiles = chosen.shape[0]
         height = tiles * ROWS
         spread = jnp.concatenate(
             [
                 jnp.where(chosen, part[None], 0.0).reshape(height, total).astype(BF16)
-                for part in parts_of(value, number)
+                for part in parts
             ],
             axis=0,
         )
         placed = matmul(spread, lane_hot, ((1,), (1,)))
         merged = placed[:height]
-        for at in range(1, number):
+        for at in range(1, len(parts)):
             merged = merged + placed[at * height : (at + 1) * height]
         return merged.reshape(tiles, ROWS, LANES)
 
@@ -159,17 +164,18 @@
                     cell_ref[axis, k, pl.ds(s, 1), :].astype(F32)
                     + frac_ref[axis, k, pl.ds(s, 1), :]
                 )
-    tiles = scatter(payload[...], whole, 3)
-    out_a[...] = tiles[:, : 2 * orients]
-    in_a[0] = tiles[0, : 2 * orients]
-
-    pl.semaphore_wait(barrier, count - 1)
-
-    chunks = slots // CHUNK
-    edges = [0, chunks // 2 * CHUNK, slots]
+    edges = [0, slots // 2, slots]
     reach = [1] + [min(count, (stop - 1) // width + 1) for stop in edges[1:]]
+    ready = [0, edges[1] // width // 2 * 2, count]
+    payload_parts = parts_of(payload[...], 3)
     for part in range(2):
-        spread_out(0, part, out_a, in_a, ahead, reach[part], reach[part + 1])
+        start, stop = (0, reach[1]) if part == 0 else (reach[1], count)
+        tiles = scatter(payload_parts, whole(start, stop))
+        out_a[pl.ds(start, stop - start)] = tiles[:, : 2 * orients]
+        if part == 0:
+            in_a[0] = tiles[0, : 2 * orients]
+            pl.semaphore_wait(barrier, count - 1)
+        spread_out(0, part, out_a, in_a, ahead, max(start, 1), stop)
 
     load_planes.wait()
     load_first.wait()
@@ -186,8 +192,8 @@
 
     row = lax.broadcasted_iota(jnp.int32, (ROWS, LANES), 0)
     lane = lax.broadcasted_iota(jnp.int32, (ROWS, LANES), 1)
-    lines = lax.broadcasted_iota(jnp.int32, (side, CHUNK), 0).astype(F32)
-    chunk_row = lax.broadcasted_iota(jnp.int32, (ROWS, CHUNK), 0)
+    lines = lax.broadcasted_iota(jnp.int32, (side, slots // 2), 0).astype(F32)
+    half_row = lax.broadcasted_iota(jnp.int32, (ROWS, slots // 2), 0)
 
     def moved(tile, amount):
         return pltpu.roll(tile, amount % LANES, 1) if amount % LANES else tile
@@ -220,8 +226,8 @@
                 )
         return value
 
-    def forward(chunk, carry):
-        lanes = pl.ds(pl.multiple_of(chunk * CHUNK, CHUNK), CHUNK)
+    def forward(part):
+        lanes = pl.ds(edges[part], slots // 2)
         for b in range(bricks):
             for orient in range(orients):
                 near_a = jnp.maximum(
@@ -232,7 +238,7 @@
                 )
                 weights = near_a[:, None, :] * near_b[None, :, :]
                 corner[b, pl.ds(orient * cells, cells), lanes] = weights.reshape(
-                    cells, CHUNK
+                    cells, slots // 2
                 ).astype(BF16)
             mixed = matmul(planes_t[b], corner[b, :, lanes], ((1,), (0,))).astype(BF16)
             feature[b, :, lanes] = mixed
@@ -242,11 +248,9 @@
             raw = matmul(last_wide[b].astype(BF16), active, ((1,), (0,)))
             gate = jax.nn.sigmoid(raw)
             soft = jnp.maximum(raw, 0.0) + jnp.log1p(jnp.exp(-jnp.abs(raw)))
-            answers[b, :, lanes] = jnp.where(chunk_row == 0, soft, gate)
-            slope[b, :, lanes] = jnp.where(chunk_row == 0, gate, gate * (1.0 - gate))
-        return carry
-
-    returned = 0
+            answers[b, :, lanes] = jnp.where(half_row == 0, soft, gate)
+            slope[b, :, lanes] = jnp.where(half_row == 0, gate, gate * (1.0 - gate))
+
     for part in range(2):
         gather_in(0, part, out_a, in_a, reach[part], reach[part + 1])
         for b in range(bricks):
@@ -254,24 +258,26 @@
                 spots[b, pl.ds(0, 2 * orients), pl.ds(block * LANES, LANES)] = columns(
                     in_a, b, block
                 )
-        lax.fori_loop(edges[part] // CHUNK, edges[part + 1] // CHUNK, forward, 0)
-        ready = min(count, edges[part + 1] // width)
-        for t in range(returned, ready):
+        forward(part)
+        for t in range(ready[part], ready[part + 1]):
             out_b[t] = tile_of(answers, t)[:HALF]
-        spread_out(1, 0, out_b, in_b, behind, max(returned, 1), ready)
-        returned = ready
+        spread_out(1, part, out_b, in_b, behind, max(ready[part], 1), ready[part + 1])
     in_b[0] = out_b[0]
     sent(0, out_a, in_a)
-    gather_in(1, 0, out_b, in_b, 1, count)
-
-    held = jnp.concatenate([in_b[t] for t in range(count)], axis=0)
-    found = matmul(
-        jnp.concatenate([part.astype(BF16) for part in parts_of(held, 2)], axis=0),
-        lane_hot,
-        ((1,), (0,)),
-    )
-    found = (found[: count * HALF] + found[count * HALF :]).reshape(halves_of)
-    found = jnp.sum(jnp.where(paired, found, 0.0), axis=0)
+
+    found = jnp.zeros((ROWS, total), F32)
+    for part in range(2):
+        start, stop = ready[part], ready[part + 1]
+        gather_in(1, part, out_b, in_b, max(start, 1), stop)
+        held = jnp.concatenate([in_b[t] for t in range(start, stop)], axis=0)
+        taken = matmul(
+            jnp.concatenate([value.astype(BF16) for value in parts_of(held, 2)], axis=0),
+            lane_hot,
+            ((1,), (0,)),
+        )
+        height = (stop - start) * HALF
+        taken = (taken[:height] + taken[height:]).reshape(height // ROWS, ROWS, total)
+        found = found + jnp.sum(jnp.where(paired(start, stop), taken, 0.0), axis=0)
     found = found[:HALF] + found[HALF:]
     found = jnp.concatenate([found, found], axis=0)
     views = [found[:, i * rays : (i + 1) * rays] for i in range(points)]
@@ -297,18 +303,15 @@
         density_cot = (passed[i] * shade_dot - behind_sum) * lengths[i]
         behind_sum = behind_sum + weights[i] * shade_dot
         cotangents[i] = jnp.where((row & 3) == 0, density_cot, weights[i] * residual)
-    tiles = scatter(jnp.concatenate(cotangents, axis=1), paired, 2)
-    for t in range(count):
-        out_c[t] = tiles[t // 2, (t % 2) * HALF : (t % 2 + 1) * HALF]
+    cotangent_parts = parts_of(jnp.concatenate(cotangents, axis=1), 2)
+    middle = count // 2
+    for start, stop in ((middle, count), (0, middle)):
+        tiles = scatter(cotangent_parts, paired(start, stop))
+        for t in range(start, stop):
+            at = t - start
+            out_c[t] = tiles[at // 2, (at % 2) * HALF : (at % 2 + 1) * HALF]
+        spread_out(2, 0, out_c, in_c, ahead, max(start, 1), stop)
     in_c[0] = out_c[0]
-
-    def send_c(turn, carry):
-        offset = turn + count // 2 - 1
-        offset = jnp.where(offset >= count, offset - (count - 1), offset)
-        transfer(2, 0, out_c, in_c, offset, ahead(offset)).start()
-        return carry
-
-    lax.fori_loop(1, count, send_c, 0)
     sent(1, out_b, in_b)
     gather_in(2, 0, out_c, in_c, 1, count)
     sent(2, out_c, in_c)

time: 35.8 us -> 31.6 us (0.88)
  Pallas kernels: 35 us -> 30.8 us
    pallas_call x1, Pallas kernels: 28.6 us -> 24.4 us  [on_device(): pl.pallas_call(functools.partial(step_kernel, along_x, along_y, capacity)...]
where the time goes in v4:
time: 31.6 us; the launch traced here: 31.4 us
  Pallas kernels  30.8 us (97%)
  between operations  0.64 us (2%)
    pallas_call x1, Pallas kernels, on_device(): pl.pallas_call(functools.partial(step_kernel, along_x, along_y, capacity)...  24.4 us
    pallas_call x1, Pallas kernels, on_device(): pl.pallas_call(gradient_kernel, out_shape=[jax.ShapeDtypeStruct(shape, F3...  6.42 us

profile of v4, /device:TPU:0, one launch (start us, length us, event | category | flops | bytes accessed | tf_op | source)
XLA Modules:
  0.0 31.4 jit_solution(15533211405772267521)
XLA Ops:
  0.6 24.4 %shard_map.111 = (f32[3,128]{1,0:T(4,128)S(1)}, bf16[2,768,1792]{2,1,0:T(8,128)(2,1)S(1)}, bf16[2,128,1792]{2,1,0:T(8,128)(2,1)S(1)}, bf16[2,256,1792]{2,1,0:T(8...) custom-call(s32[3,128]{1,0:T(4,128)} %bitcast.2, ...), custom_call_target="tpu_custom_call" | custom-call | tf_op jit(solution)/shard_map/pallas_call | solution.py:395
  25.0 6.4 %shard_map.112 = (f32[3,128]{1,0:T(4,128)}, f32[2,768,128]{2,1,0:T(8,128)}, f32[2,128,256]{2,1,0:T(8,128)}, f32[2,4,256]{2,1,0:T(4,128)}) custom-call(f32[3,128]{1,0:T(4,128)S(1)} %get-tuple-element.15.colour_in, bf16[2,768,1792]{2,1,0:T(8,128)(2,1)S(1)} %get-tuple-element.16.corner, bf16[2,128,1792]{2,1,0:T(8,128)(2,1)S(1)} %get-tuple-element.17.feature, ...), custom_call_target="tpu_custom_call" | custom-call | tf_op jit(solution)/shard_map/pallas_call | solution.py:424

commit v5 on v4

--- a/solution.py
+++ b/solution.py
@@ -27,6 +27,11 @@
         parts.append(part)
         value = value - part
     return parts + [value]
+
+
+def column_edges(slots):
+    first = (slots // 2 + CHUNK - 1) // CHUNK * CHUNK
+    return [0, first, slots]
 
 
 def step_kernel(
@@ -164,9 +169,9 @@
                     cell_ref[axis, k, pl.ds(s, 1), :].astype(F32)
                     + frac_ref[axis, k, pl.ds(s, 1), :]
                 )
-    edges = [0, slots // 2, slots]
+    edges = column_edges(slots)
     reach = [1] + [min(count, (stop - 1) // width + 1) for stop in edges[1:]]
-    ready = [0, edges[1] // width // 2 * 2, count]
+    ready = [0, edges[1] // width // 4 * 4, count]
     payload_parts = parts_of(payload[...], 3)
     for part in range(2):
         start, stop = (0, reach[1]) if part == 0 else (reach[1], count)
@@ -192,8 +197,6 @@
 
     row = lax.broadcasted_iota(jnp.int32, (ROWS, LANES), 0)
     lane = lax.broadcasted_iota(jnp.int32, (ROWS, LANES), 1)
-    lines = lax.broadcasted_iota(jnp.int32, (side, slots // 2), 0).astype(F32)
-    half_row = lax.broadcasted_iota(jnp.int32, (ROWS, slots // 2), 0)
 
     def moved(tile, amount):
         return pltpu.roll(tile, amount % LANES, 1) if amount % LANES else tile
@@ -227,7 +230,10 @@
         return value
 
     def forward(part):
-        lanes = pl.ds(edges[part], slots // 2)
+        span = edges[part + 1] - edges[part]
+        lanes = pl.ds(edges[part], span)
+        lines = lax.broadcasted_iota(jnp.int32, (side, span), 0).astype(F32)
+        span_row = lax.broadcasted_iota(jnp.int32, (ROWS, span), 0)
         for b in range(bricks):
             for orient in range(orients):
                 near_a = jnp.maximum(
@@ -238,7 +244,7 @@
                 )
                 weights = near_a[:, None, :] * near_b[None, :, :]
                 corner[b, pl.ds(orient * cells, cells), lanes] = weights.reshape(
-                    cells, slots // 2
+                    cells, span
                 ).astype(BF16)
             mixed = matmul(planes_t[b], corner[b, :, lanes], ((1,), (0,))).astype(BF16)
             feature[b, :, lanes] = mixed
@@ -248,8 +254,8 @@
             raw = matmul(last_wide[b].astype(BF16), active, ((1,), (0,)))
             gate = jax.nn.sigmoid(raw)
             soft = jnp.maximum(raw, 0.0) + jnp.log1p(jnp.exp(-jnp.abs(raw)))
-            answers[b, :, lanes] = jnp.where(half_row == 0, soft, gate)
-            slope[b, :, lanes] = jnp.where(half_row == 0, gate, gate * (1.0 - gate))
+            answers[b, :, lanes] = jnp.where(span_row == 0, soft, gate)
+            slope[b, :, lanes] = jnp.where(span_row == 0, gate, gate * (1.0 - gate))
 
     for part in range(2):
         gather_in(0, part, out_a, in_a, reach[part], reach[part + 1])
@@ -340,26 +346,22 @@
             for at, (source, landing) in enumerate(pairs)
         ]
 
-    def one_brick(b, carry):
+    edges = column_edges(slots)
+    for b in range(bricks):
         cot = raw_cot[b].astype(BF16)
-        for chunk in range(slots // CHUNK):
-            lanes = pl.ds(chunk * CHUNK, CHUNK)
-            pull = matmul(
-                last_wide[b].astype(BF16),
-                cot[:, chunk * CHUNK : (chunk + 1) * CHUNK],
-                ((0,), (0,)),
-            )
+        for start, stop in zip(edges, edges[1:]):
+            lanes = pl.ds(start, stop - start)
+            pull = matmul(last_wide[b].astype(BF16), cot[:, start:stop], ((0,), (0,)))
             masked = jnp.where(hidden[b, :, lanes].astype(F32) > 0.0, pull, 0.0).astype(BF16)
-            before_cot[:, lanes] = masked
-            feature_cot[:, lanes] = matmul(first_ref[b], masked, ((1,), (0,))).astype(BF16)
-        plane_part[b] = matmul(corner[b], feature_cot[...], ((1,), (1,)))
-        first_part[b] = matmul(feature[b], before_cot[...], ((1,), (1,)))
+            before_cot[b, :, lanes] = masked
+            feature_cot[b, :, lanes] = matmul(first_ref[b], masked, ((1,), (0,))).astype(BF16)
+        plane_copy, first_copy, last_copy = result_copies(b)
+        plane_part[b] = matmul(corner[b], feature_cot[b], ((1,), (1,)))
+        plane_copy.start()
+        first_part[b] = matmul(feature[b], before_cot[b], ((1,), (1,)))
+        first_copy.start()
         last_part[b] = matmul(cot, hidden[b], ((1,), (1,)))[:HALF]
-        for copy in result_copies(b):
-            copy.start()
-        return carry
-
-    lax.fori_loop(0, bricks, one_brick, 0)
+        last_copy.start()
     colour_copy.wait()
     for b in range(bricks):
         for copy in result_copies(b):
@@ -433,8 +435,8 @@
             pltpu.VMEM(flat, F32),
             pltpu.VMEM(first_layer.shape, F32),
             pltpu.VMEM(last_layer.shape, F32),
-            pltpu.VMEM((units, slots), BF16),
-            pltpu.VMEM((channels, slots), BF16),
+            pltpu.VMEM((bricks, units, slots), BF16),
+            pltpu.VMEM((bricks, channels, slots), BF16),
             pltpu.SemaphoreType.DMA((bricks, 4)),
         ],
         compiler_params=pltpu.CompilerParams(vmem_limit_bytes=limit),

time: 31.6 us -> 29.8 us (0.943)
  Pallas kernels: 30.8 us -> 29 us
    pallas_call x1, Pallas kernels: 6.42 us -> 4.63 us  [on_device(): pl.pallas_call(gradient_kernel, out_shape=[jax.ShapeDtypeStruct(shape, F3...]
where the time goes in v5:
time: 29.8 us; the launch traced here: 29.7 us
  Pallas kernels  29 us (97%)
  between operations  0.64 us (2%)
    pallas_call x1, Pallas kernels, on_device(): pl.pallas_call(functools.partial(step_kernel, along_x, along_y, capacity)...  24.4 us
    pallas_call x1, Pallas kernels, on_device(): pl.pallas_call(gradient_kernel, out_shape=[jax.ShapeDtypeStruct(shape, F3...  4.63 us

profile of v5, /device:TPU:0, one launch (start us, length us, event | category | flops | bytes accessed | tf_op | source)
XLA Modules:
  0.0 29.7 jit_solution(1426824764549903281)
XLA Ops:
  0.6 24.4 %shard_map.111 = (f32[3,128]{1,0:T(4,128)S(1)}, bf16[2,768,1792]{2,1,0:T(8,128)(2,1)S(1)}, bf16[2,128,1792]{2,1,0:T(8,128)(2,1)S(1)}, bf16[2,256,1792]{2,1,0:T(8...) custom-call(s32[3,128]{1,0:T(4,128)} %bitcast.2, ...), custom_call_target="tpu_custom_call" | custom-call | tf_op jit(solution)/shard_map/pallas_call | solution.py:397
  25.0 4.6 %shard_map.112 = (f32[3,128]{1,0:T(4,128)}, f32[2,768,128]{2,1,0:T(8,128)}, f32[2,128,256]{2,1,0:T(8,128)}, f32[2,4,256]{2,1,0:T(4,128)}) custom-call(f32[3,128]{1,0:T(4,128)S(1)} %get-tuple-element.15.colour_in, bf16[2,768,1792]{2,1,0:T(8,128)(2,1)S(1)} %get-tuple-element.16.corner, bf16[2,128,1792]{2,1,0:T(8,128)(2,1)S(1)} %get-tuple-element.17.feature, ...), custom_call_target="tpu_custom_call" | custom-call | tf_op jit(solution)/shard_map/pallas_call | solution.py:426

commit v6 on v5

--- a/solution.py
+++ b/solution.py
@@ -59,8 +59,6 @@
 
     load_planes = pltpu.make_async_copy(planes_hbm, planes_ref, load_sem.at[0])
     load_first = pltpu.make_async_copy(first_hbm, first_ref, load_sem.at[1])
-    load_planes.start()
-    load_first.start()
 
     shift_y = along_y.bit_length() - 1
 
@@ -104,7 +102,9 @@
         pl.semaphore_signal(barrier, inc=1, device_id=ahead(offset), device_id_type=MESH)
         return carry
 
-    lax.fori_loop(1, count, greet, 0)
+    lax.fori_loop(1, count, greet, 0, unroll=True)
+    load_planes.start()
+    load_first.start()
 
     ids = [ids_ref[pl.ds(k, 1), :] for k in range(crossed)]
     ids_row = jnp.concatenate(ids, axis=1)

time: 29.8 us -> 29.8 us (level)
  no operation moved by 1% of the time
where the time goes in v6:
time: 29.8 us; the launch traced here: 29.7 us
  Pallas kernels  29 us (97%)
  between operations  0.64 us (2%)
    pallas_call x1, Pallas kernels, on_device(): pl.pallas_call(functools.partial(step_kernel, along_x, along_y, capacity)...  24.4 us
    pallas_call x1, Pallas kernels, on_device(): pl.pallas_call(gradient_kernel, out_shape=[jax.ShapeDtypeStruct(shape, F3...  4.63 us

profile of v6, /device:TPU:0, one launch (start us, length us, event | category | flops | bytes accessed | tf_op | source)
XLA Modules:
  0.0 29.7 jit_solution(9550276102068323618)
XLA Ops:
  0.6 24.4 %shard_map.111 = (f32[3,128]{1,0:T(4,128)S(1)}, bf16[2,768,1792]{2,1,0:T(8,128)(2,1)S(1)}, bf16[2,128,1792]{2,1,0:T(8,128)(2,1)S(1)}, bf16[2,256,1792]{2,1,0:T(8...) custom-call(s32[3,128]{1,0:T(4,128)} %bitcast.2, ...), custom_call_target="tpu_custom_call" | custom-call | tf_op jit(solution)/shard_map/pallas_call | solution.py:397
  25.0 4.6 %shard_map.112 = (f32[3,128]{1,0:T(4,128)}, f32[2,768,128]{2,1,0:T(8,128)}, f32[2,128,256]{2,1,0:T(8,128)}, f32[2,4,256]{2,1,0:T(4,128)}) custom-call(f32[3,128]{1,0:T(4,128)S(1)} %get-tuple-element.15.colour_in, bf16[2,768,1792]{2,1,0:T(8,128)(2,1)S(1)} %get-tuple-element.16.corner, bf16[2,128,1792]{2,1,0:T(8,128)(2,1)S(1)} %get-tuple-element.17.feature, ...), custom_call_target="tpu_custom_call" | custom-call | tf_op jit(solution)/shard_map/pallas_call | solution.py:426
